TPU v7x, 32 devices: a whole 2x2x4 slice. The times are simulated.
32 devices in a mesh: dp: 8 (over z, x), fsdp: 4 (over y, core).
Axes of the slice: x: 2, y: 2, z: 4, core: 2. Of those that a mesh axis runs over, the one named last changes fastest.
Arguments:
- tokens: bfloat16 [4, 64, 512, 512], P(None, ('dp', 'fsdp'))
- memory_state: bfloat16 [4, 64, 20, 512], P(None, ('dp', 'fsdp')), may hold values from -6 to 6
- cotangent: bfloat16 [4, 64, 532, 512], P(None, ('dp', 'fsdp')), may hold values from -6 to 6
- in_weight: float32 [512, 1536], P(('dp', 'fsdp')), may hold values from -0.25 to 0.25
- in_first: float32 [512, 1536], P(('dp', 'fsdp')), may hold values from -0.0034179688 to 0.0034179688
- in_second: float32 [512, 1536], P(('dp', 'fsdp')), may hold values from 3.1624432e-07 to 1.2649773e-06
- out_weight: float32 [512, 512], P(None, ('dp', 'fsdp')), may hold values from -1 to 1
- out_first: float32 [512, 512], P(None, ('dp', 'fsdp')), may hold values from -0.0034179688 to 0.0034179688
- out_second: float32 [512, 512], P(None, ('dp', 'fsdp')), may hold values from 3.1624432e-07 to 1.2649773e-06
- up_weight: float32 [512, 2048], P(('dp', 'fsdp')), may hold values from -0.25 to 0.25
- up_first: float32 [512, 2048], P(('dp', 'fsdp')), may hold values from -0.0034179688 to 0.0034179688
- up_second: float32 [512, 2048], P(('dp', 'fsdp')), may hold values from 3.1624432e-07 to 1.2649773e-06
- down_weight: float32 [2048, 512], P(None, ('dp', 'fsdp')), may hold values from -0.125 to 0.125
- down_first: float32 [2048, 512], P(None, ('dp', 'fsdp')), may hold values from -0.0034179688 to 0.0034179688
- down_second: float32 [2048, 512], P(None, ('dp', 'fsdp')), may hold values from 3.1624432e-07 to 1.2649773e-06
- vectors: float32 [8, 512], P(None, ('dp', 'fsdp'))
- vectors_first: float32 [8, 512], P(None, ('dp', 'fsdp')), may hold values from -0.0034179688 to 0.0034179688
- vectors_second: float32 [8, 512], P(None, ('dp', 'fsdp')), may hold values from 3.1624432e-07 to 1.2649773e-06
- up_bias: float32 [2048], P(('dp', 'fsdp')), may hold values from -1.75 to 1.75
- up_bias_first: float32 [2048], P(('dp', 'fsdp')), may hold values from -0.0034179688 to 0.0034179688
- up_bias_second: float32 [2048], P(('dp', 'fsdp')), may hold values from 3.1624432e-07 to 1.2649773e-06
- memory_embed: float32 [20, 512], P(None, ('dp', 'fsdp')), may hold values from -6 to 6
- memory_first: float32 [20, 512], P(None, ('dp', 'fsdp')), may hold values from -0.00061035156 to 0.00061035156
- memory_second: float32 [20, 512], P(None, ('dp', 'fsdp')), may hold values from 1.18888845e-08 to 4.7555538e-08
Outputs:
- output: bfloat16 [4, 64, 532, 512], P(None, ('dp', 'fsdp'))
- input_grad: float32 [4, 64, 512, 512], P(None, ('dp', 'fsdp'))
- in_weight_new: float32 [512, 1536], P(('dp', 'fsdp'))
- in_first_new: float32 [512, 1536], P(('dp', 'fsdp'))
- in_second_new: float32 [512, 1536], P(('dp', 'fsdp'))
- out_weight_new: float32 [512, 512], P(None, ('dp', 'fsdp'))
- out_first_new: float32 [512, 512], P(None, ('dp', 'fsdp'))
- out_second_new: float32 [512, 512], P(None, ('dp', 'fsdp'))
- up_weight_new: float32 [512, 2048], P(('dp', 'fsdp'))
- up_first_new: float32 [512, 2048], P(('dp', 'fsdp'))
- up_second_new: float32 [512, 2048], P(('dp', 'fsdp'))
- down_weight_new: float32 [2048, 512], P(None, ('dp', 'fsdp'))
- down_first_new: float32 [2048, 512], P(None, ('dp', 'fsdp'))
- down_second_new: float32 [2048, 512], P(None, ('dp', 'fsdp'))
- vectors_new: float32 [8, 512], P(None, ('dp', 'fsdp'))
- vectors_first_new: float32 [8, 512], P(None, ('dp', 'fsdp'))
- vectors_second_new: float32 [8, 512], P(None, ('dp', 'fsdp'))
- up_bias_new: float32 [2048], P(('dp', 'fsdp'))
- up_bias_first_new: float32 [2048], P(('dp', 'fsdp'))
- up_bias_second_new: float32 [2048], P(('dp', 'fsdp'))
- memory_embed_new: float32 [20, 512], P(None, ('dp', 'fsdp'))
- memory_first_new: float32 [20, 512], P(None, ('dp', 'fsdp'))
- memory_second_new: float32 [20, 512], P(None, ('dp', 'fsdp'))
- grad_norm: float32 [], replicated
All inputs are finite; a program needn't handle non-finite values.
Results may differ from a plain program's by a relative error of at most 0.012.
The roundings to bfloat16 on the way count: a program that leaves them out, or rounds other values in their place, can miss the bound.
Values may be sent and summed in bfloat16 or wider, within the bound.
No kernel may reach another device: no remote copies, remote signals or barrier semaphores. Data moves between devices by JAX's collectives and lax.ppermute only.
A program may use at most 192 MiB of HBM per device.

v0:
```python
from functools import partial

import jax
import jax.numpy as jnp
from jax import lax
from jax.sharding import PartitionSpec as P

D = 512
FF = 2048
MEM = 20
SEQ = 512
STEP = 7
HDIM = 64


norm_eps = 1e-05
clip_level = 1.0


def normalize(value, gain, shift):
    center = value - jnp.mean(value, axis=-1, keepdims=True)
    rstd = lax.rsqrt(jnp.mean(center * center, axis=-1, keepdims=True) + norm_eps)
    normed = center * rstd
    return (normed * gain + shift, normed, rstd)


def norm_back(grad, normed, rstd, gain):
    scaled = grad * gain
    return rstd * (
        scaled
        - jnp.mean(scaled, axis=-1, keepdims=True)
        - normed * jnp.mean(scaled * normed, axis=-1, keepdims=True)
    )


def row_total(value):
    return jnp.sum(value.astype(jnp.float32), axis=(0, 1))


def split_heads(value, heads):
    count, length, width = value.shape
    return value.reshape(count, length, heads, width // heads)


def scores_of(query, keys, allowed):
    raw = jnp.einsum("cqhe,ckhe->chqk", query, keys, preferred_element_type=jnp.float32) * HDIM ** (
        -0.5
    )
    return jnp.where(allowed, raw, -1e30)


def forward(params, full, allowed):
    in_w, out_w, up_w, down_w, vecs, up_b = params
    vecf = vecs.astype(jnp.float32)
    width = out_w.shape[0]
    heads = width // HDIM
    inputs = full.astype(jnp.bfloat16)
    joint = jnp.einsum("csd,de->cse", inputs, in_w, preferred_element_type=jnp.float32)
    query = (joint[..., :width] + vecf[0]).astype(jnp.bfloat16)
    keys = joint[..., width : 2 * width].astype(jnp.bfloat16)
    values = (joint[..., 2 * width :] + vecf[1]).astype(jnp.bfloat16)
    scores = scores_of(split_heads(query, heads), split_heads(keys, heads), allowed)
    top = jnp.max(scores, axis=-1, keepdims=True)
    expo = jnp.exp(scores - top)
    total = jnp.sum(expo, axis=-1, keepdims=True)
    probs = (expo / total).astype(jnp.bfloat16)
    logsum = top + jnp.log(total)
    mixed = (
        jnp.einsum(
            "chqk,ckhe->cqhe", probs, split_heads(values, heads), preferred_element_type=jnp.float32
        )
        .reshape(full.shape)
        .astype(jnp.bfloat16)
    )
    attended = jnp.einsum("csd,de->cse", mixed, out_w, preferred_element_type=jnp.float32) + vecf[2]
    first, normed_one, rstd_one = normalize(full + attended, vecf[4], vecf[5])
    first_low = first.astype(jnp.bfloat16)
    hidden_pre = jnp.einsum(
        "csd,df->csf", first_low, up_w, preferred_element_type=jnp.float32
    ) + up_b.astype(jnp.float32)
    hidden = jax.nn.gelu(hidden_pre, approximate=True).astype(jnp.bfloat16)
    branch = jnp.einsum("csf,fd->csd", hidden, down_w, preferred_element_type=jnp.float32) + vecf[3]
    output, normed_two, rstd_two = normalize(first + branch, vecf[6], vecf[7])
    kept = (
        inputs,
        query,
        keys,
        values,
        logsum,
        mixed,
        normed_one,
        rstd_one,
        first_low,
        hidden_pre,
        hidden,
        normed_two,
        rstd_two,
    )
    return (output, kept)


def backward(params, kept, grad_out, allowed):
    in_w, out_w, up_w, down_w, vecs, up_b = params
    vecf = vecs.astype(jnp.float32)
    (
        inputs,
        query,
        keys,
        values,
        logsum,
        mixed,
        normed_one,
        rstd_one,
        first_low,
        hidden_pre,
        hidden,
        normed_two,
        rstd_two,
    ) = kept
    count, length, width = inputs.shape
    heads = width // HDIM
    gain_two = row_total(grad_out * normed_two)
    shift_two = row_total(grad_out)
    grad_two = norm_back(grad_out, normed_two, rstd_two, vecf[6])
    grad_branch = grad_two.astype(jnp.bfloat16)
    grad_down = jnp.einsum("csf,csd->fd", hidden, grad_branch, preferred_element_type=jnp.float32)
    grad_hidden = jnp.einsum("csd,fd->csf", grad_branch, down_w, preferred_element_type=jnp.float32)
    unused, gelu_pull = jax.vjp(partial(jax.nn.gelu, approximate=True), hidden_pre)
    grad_pre = gelu_pull(grad_hidden)[0].astype(jnp.bfloat16)
    grad_up = jnp.einsum("csd,csf->df", first_low, grad_pre, preferred_element_type=jnp.float32)
    grad_first = grad_two + jnp.einsum(
        "csf,df->csd", grad_pre, up_w, preferred_element_type=jnp.float32
    )
    gain_one = row_total(grad_first * normed_one)
    shift_one = row_total(grad_first)
    grad_one = norm_back(grad_first, normed_one, rstd_one, vecf[4])
    grad_att = grad_one.astype(jnp.bfloat16)
    grad_outw = jnp.einsum("csd,cse->de", mixed, grad_att, preferred_element_type=jnp.float32)
    grad_mixed = jnp.einsum(
        "cse,de->csd", grad_att, out_w, preferred_element_type=jnp.float32
    ).astype(jnp.bfloat16)
    grad_mixed = split_heads(grad_mixed, heads)
    query_heads = split_heads(query, heads)
    key_heads = split_heads(keys, heads)
    value_heads = split_heads(values, heads)
    probs = jnp.exp(scores_of(query_heads, key_heads, allowed) - logsum)
    grad_probs = jnp.einsum(
        "cqhe,ckhe->chqk", grad_mixed, value_heads, preferred_element_type=jnp.float32
    )
    grad_scores = probs * (grad_probs - jnp.sum(grad_probs * probs, axis=-1, keepdims=True))
    grad_scores = grad_scores.astype(jnp.bfloat16)
    scale = HDIM ** (-0.5)
    grad_query = (
        jnp.einsum("chqk,ckhe->cqhe", grad_scores, key_heads, preferred_element_type=jnp.float32)
        * scale
    ).astype(jnp.bfloat16)
    grad_keys = (
        jnp.einsum("chqk,cqhe->ckhe", grad_scores, query_heads, preferred_element_type=jnp.float32)
        * scale
    ).astype(jnp.bfloat16)
    grad_values = jnp.einsum(
        "chqk,cqhe->ckhe",
        probs.astype(jnp.bfloat16),
        grad_mixed,
        preferred_element_type=jnp.float32,
    ).astype(jnp.bfloat16)
    grad_query = grad_query.reshape(count, length, width)
    grad_keys = grad_keys.reshape(count, length, width)
    grad_values = grad_values.reshape(count, length, width)
    grad_joint = jnp.concatenate([grad_query, grad_keys, grad_values], axis=-1)
    grad_in = jnp.einsum("csd,cse->de", inputs, grad_joint, preferred_element_type=jnp.float32)
    grad_full = grad_one + jnp.einsum(
        "cse,de->csd", grad_joint, in_w, preferred_element_type=jnp.float32
    )
    grad_vec = jnp.stack(
        [
            row_total(grad_query),
            row_total(grad_values),
            row_total(grad_att),
            row_total(grad_branch),
            gain_one,
            shift_one,
            gain_two,
            shift_two,
        ]
    )
    grad_upb = row_total(grad_pre)
    return (grad_full, (grad_in, grad_outw, grad_up, grad_down, grad_vec, grad_upb))


def adam_step(weight, first, second, grad, rate, decay):
    first_new = 0.5 * first + 0.5 * grad
    second_new = 0.5 * second + 0.5 * grad * grad
    correction = 1.0 - 0.5**STEP
    weight_new = weight - rate * (
        first_new / correction / (jnp.sqrt(second_new / correction) + 1e-08) + decay * weight
    )
    return (weight_new, first_new, second_new)


def per_device(
    tokens,
    memory_state,
    cotangent,
    in_weight,
    in_first,
    in_second,
    out_weight,
    out_first,
    out_second,
    up_weight,
    up_first,
    up_second,
    down_weight,
    down_first,
    down_second,
    vectors,
    vectors_first,
    vectors_second,
    up_bias,
    up_bias_first,
    up_bias_second,
    memory_embed,
    memory_first,
    memory_second,
):
    extra = memory_state.shape[2]
    length = extra + tokens.shape[2]
    place = jnp.arange(length)
    allowed = (
        (place[None, :] < extra) | (place[:, None] < extra) | (place[None, :] <= place[:, None])
    )
    masters = (in_weight, out_weight, up_weight, down_weight, vectors, up_bias, memory_embed)
    lowered = tuple((weight.astype(jnp.bfloat16) for weight in masters))
    start = tuple((jnp.zeros(weight.shape, jnp.float32) for weight in masters))

    def micro_step(carry, items):
        batch_tokens, batch_state, batch_cot = items
        gathered = (
            lax.all_gather(lowered[0], ("dp", "fsdp"), axis=0, tiled=True),
            lax.all_gather(lowered[1], ("dp", "fsdp"), axis=1, tiled=True),
            lax.all_gather(lowered[2], ("dp", "fsdp"), axis=0, tiled=True),
            lax.all_gather(lowered[3], ("dp", "fsdp"), axis=1, tiled=True),
            lax.all_gather(lowered[4], ("dp", "fsdp"), axis=1, tiled=True),
            lax.all_gather(lowered[5], ("dp", "fsdp"), axis=0, tiled=True),
            lax.all_gather(lowered[6], ("dp", "fsdp"), axis=1, tiled=True),
        )
        params = gathered[:6]
        memory_rows = gathered[6].astype(jnp.float32)[None] + batch_state.astype(jnp.float32)
        full = jnp.concatenate([memory_rows, batch_tokens.astype(jnp.float32)], axis=1)
        output, kept = forward(params, full, allowed)
        grad_full, grads = backward(params, kept, batch_cot.astype(jnp.float32), allowed)
        grads = grads + (jnp.sum(grad_full[:, :extra, :], axis=0),)
        piece = (
            lax.psum_scatter(grads[0], ("dp", "fsdp"), scatter_dimension=0, tiled=True),
            lax.psum_scatter(grads[1], ("dp", "fsdp"), scatter_dimension=1, tiled=True),
            lax.psum_scatter(grads[2], ("dp", "fsdp"), scatter_dimension=0, tiled=True),
            lax.psum_scatter(grads[3], ("dp", "fsdp"), scatter_dimension=1, tiled=True),
            lax.psum_scatter(grads[4], ("dp", "fsdp"), scatter_dimension=1, tiled=True),
            lax.psum_scatter(grads[5], ("dp", "fsdp"), scatter_dimension=0, tiled=True),
            lax.psum_scatter(grads[6], ("dp", "fsdp"), scatter_dimension=1, tiled=True),
        )
        carry = tuple((older + newer for older, newer in zip(carry, piece)))
        return (carry, (output.astype(jnp.bfloat16), grad_full[:, extra:, :]))

    accumulated, stacked = lax.scan(micro_step, start, (tokens, memory_state, cotangent))
    outputs, input_grads = stacked
    squares = jnp.float32(0.0)
    for grad in accumulated:
        squares = squares + jnp.sum(grad * grad)
    total = lax.psum(squares, ("dp", "fsdp"))
    grad_norm = jnp.sqrt(total)
    factor = clip_level / jnp.maximum(grad_norm, clip_level)
    rates = (
        0.5 * D ** (-0.5),
        0.5 * (D * 32 // (MEM + SEQ)) ** (-0.5),
        0.5 * D ** (-0.5),
        0.5 * FF ** (-0.5),
        0.1,
        0.1,
        0.5,
    )
    decays = (0.1, 0.1, 0.1, 0.1, 0.0, 0.0, 0.0)
    firsts = (in_first, out_first, up_first, down_first, vectors_first, up_bias_first, memory_first)
    seconds = (
        in_second,
        out_second,
        up_second,
        down_second,
        vectors_second,
        up_bias_second,
        memory_second,
    )
    results = []
    for index in range(7):
        results.extend(
            adam_step(
                masters[index],
                firsts[index],
                seconds[index],
                accumulated[index] * factor,
                rates[index],
                decays[index],
            )
        )
    return (
        outputs,
        input_grads,
        results[0],
        results[1],
        results[2],
        results[3],
        results[4],
        results[5],
        results[6],
        results[7],
        results[8],
        results[9],
        results[10],
        results[11],
        results[12],
        results[13],
        results[14],
        results[15],
        results[16],
        results[17],
        results[18],
        results[19],
        results[20],
        grad_norm,
    )


def solution(mesh):
    in_specs = (
        P(None, ("dp", "fsdp"), None, None),
        P(None, ("dp", "fsdp"), None, None),
        P(None, ("dp", "fsdp"), None, None),
        P(("dp", "fsdp"), None),
        P(("dp", "fsdp"), None),
        P(("dp", "fsdp"), None),
        P(None, ("dp", "fsdp")),
        P(None, ("dp", "fsdp")),
        P(None, ("dp", "fsdp")),
        P(("dp", "fsdp"), None),
        P(("dp", "fsdp"), None),
        P(("dp", "fsdp"), None),
        P(None, ("dp", "fsdp")),
        P(None, ("dp", "fsdp")),
        P(None, ("dp", "fsdp")),
        P(None, ("dp", "fsdp")),
        P(None, ("dp", "fsdp")),
        P(None, ("dp", "fsdp")),
        P(("dp", "fsdp")),
        P(("dp", "fsdp")),
        P(("dp", "fsdp")),
        P(None, ("dp", "fsdp")),
        P(None, ("dp", "fsdp")),
        P(None, ("dp", "fsdp")),
    )
    out_specs = (
        P(None, ("dp", "fsdp"), None, None),
        P(None, ("dp", "fsdp"), None, None),
        P(("dp", "fsdp"), None),
        P(("dp", "fsdp"), None),
        P(("dp", "fsdp"), None),
        P(None, ("dp", "fsdp")),
        P(None, ("dp", "fsdp")),
        P(None, ("dp", "fsdp")),
        P(("dp", "fsdp"), None),
        P(("dp", "fsdp"), None),
        P(("dp", "fsdp"), None),
        P(None, ("dp", "fsdp")),
        P(None, ("dp", "fsdp")),
        P(None, ("dp", "fsdp")),
        P(None, ("dp", "fsdp")),
        P(None, ("dp", "fsdp")),
        P(None, ("dp", "fsdp")),
        P(("dp", "fsdp")),
        P(("dp", "fsdp")),
        P(("dp", "fsdp")),
        P(None, ("dp", "fsdp")),
        P(None, ("dp", "fsdp")),
        P(None, ("dp", "fsdp")),
        P(),
    )
    return jax.shard_map(
        per_device, mesh=mesh, in_specs=in_specs, out_specs=out_specs, check_vma=False
    )
```

profile of v0, /device:TPU:0, one launch (start us, length us, event | category | flops | bytes accessed | tf_op | source)
XLA Modules:
  0.0 4455.9 jit_solution(6587186852678990481)
XLA Ops:
  14.5 4370.7 %while.29 = (s32[]{:T(128)}, f32[16,1536]{1,0:T(8,128)}, f32[512,16]{0,1:T(8,128)}, f32[16,2048]{1,0:T(8,128)}, f32[2048,16]{0,1:T(8,128)}, /*index=5*/f32[8,16]...) while((s32[]{:T(128)}, f32[16,1536]{1,0:T(8,128)}, ...), condition=%wide.region_29.30_spmd.clone, body=%wide.region_0.29_spmd.clone.sunk | while | flops 23857788928 | bytes 662932992 | solution.py:266
  17.7 42.2 all-reduce.5
  59.9 40.3 all-gather.3
  100.6 37.1 all_gather.53
  138.8 42.4 all_gather.54
  210.9 14.0 fusion.184
  266.3 14.8 convert_reduce_fusion.15
  281.1 15.7 multiply_reduce_fusion.20
  296.9 15.4 multiply_convert_fusion.10
  366.5 37.1 all-reduce.6
  407.2 52.9 %reduce-scatter.23.cloned.1.call-done = f32[16,8]{1,0:T(8,128)} async-done(((f32[512,8]{1,0:T(8,128)}), f32[16,8]{1,0:T(8,128)}) %reduce-scatter.23.cloned.1.call-update) | async-done | bytes 528 | tf_op jit(solution)/shard_map/while
  460.8 130.7 %reduce-scatter.25.cloned.1.call-done = f32[16,20]{1,0:T(8,128)} async-done(((f32[512,20]{1,0:T(8,128)}), f32[16,20]{1,0:T(8,128)}) %reduce-scatter.25.cloned.1.call-update) | async-done | bytes 1296 | tf_op jit(solution)/shard_map/while
  592.3 132.0 %reduce-scatter.17.cloned.1.call-done = f32[512,16]{0,1:T(8,128)} async-done(((f32[512,512]{0,1:T(8,128)}), f32[512,16]{0,1:T(8,128)}) %reduce-scatter.17.cloned.1.call-update) | async-done | bytes 32784 | tf_op jit(solution)/shard_map/while/body/eval_jaxpr/reduce_scatter | solution.py:256
  725.1 102.1 %reduce-scatter.15.cloned.1.call-done = f32[16,1536]{1,0:T(8,128)} async-done(((f32[512,1536]{1,0:T(8,128)}), f32[16,1536]{1,0:T(8,128)}) %reduce-scatter.15.cloned.1.call-update) | async-done | bytes 98320 | tf_op jit(solution)/shard_map/while/body/eval_jaxpr/reduce_scatter | solution.py:255
  828.2 141.8 %reduce-scatter.21.cloned.1.call-done = f32[2048,16]{0,1:T(8,128)} async-done(((f32[2048,512]{0,1:T(8,128)}), f32[2048,16]{0,1:T(8,128)}) %reduce-scatter.21.cloned.1.call-update) | async-done | bytes 131088 | tf_op jit(solution)/shard_map/while/body/eval_jaxpr/reduce_scatter | solution.py:258
  970.9 138.9 %reduce-scatter.19.cloned.1.call-done = f32[16,2048]{1,0:T(8,128)} async-done(((f32[512,2048]{1,0:T(8,128)}), f32[16,2048]{1,0:T(8,128)}) %reduce-scatter.19.cloned.1.call-update) | async-done | bytes 131088 | tf_op jit(solution)/shard_map/while/body/eval_jaxpr/reduce_scatter | solution.py:257
  1114.5 37.0 all-reduce.5
  1151.6 40.0 all-gather.3
  1192.0 37.2 all_gather.53
  1230.3 42.4 all_gather.54
  1302.3 14.0 fusion.184
  1357.6 14.8 convert_reduce_fusion.15
  1372.4 15.7 multiply_reduce_fusion.20
  1388.1 15.4 multiply_convert_fusion.10
  1439.6 9.8 convolution_bitcast_fusion.11
  1457.8 37.0 all-reduce.6
  1498.3 53.1 %reduce-scatter.23.cloned.1.call-done = f32[16,8]{1,0:T(8,128)} async-done(((f32[512,8]{1,0:T(8,128)}), f32[16,8]{1,0:T(8,128)}) %reduce-scatter.23.cloned.1.call-update) | async-done | bytes 528 | tf_op jit(solution)/shard_map/while
  1552.2 130.8 %reduce-scatter.25.cloned.1.call-done = f32[16,20]{1,0:T(8,128)} async-done(((f32[512,20]{1,0:T(8,128)}), f32[16,20]{1,0:T(8,128)}) %reduce-scatter.25.cloned.1.call-update) | async-done | bytes 1296 | tf_op jit(solution)/shard_map/while
  1683.8 132.0 %reduce-scatter.17.cloned.1.call-done = f32[512,16]{0,1:T(8,128)} async-done(((f32[512,512]{0,1:T(8,128)}), f32[512,16]{0,1:T(8,128)}) %reduce-scatter.17.cloned.1.call-update) | async-done | bytes 32784 | tf_op jit(solution)/shard_map/while/body/eval_jaxpr/reduce_scatter | solution.py:256
  1816.6 102.0 %reduce-scatter.15.cloned.1.call-done = f32[16,1536]{1,0:T(8,128)} async-done(((f32[512,1536]{1,0:T(8,128)}), f32[16,1536]{1,0:T(8,128)}) %reduce-scatter.15.cloned.1.call-update) | async-done | bytes 98320 | tf_op jit(solution)/shard_map/while/body/eval_jaxpr/reduce_scatter | solution.py:255
  1919.5 141.3 %reduce-scatter.21.cloned.1.call-done = f32[2048,16]{0,1:T(8,128)} async-done(((f32[2048,512]{0,1:T(8,128)}), f32[2048,16]{0,1:T(8,128)}) %reduce-scatter.21.cloned.1.call-update) | async-done | bytes 131088 | tf_op jit(solution)/shard_map/while/body/eval_jaxpr/reduce_scatter | solution.py:258
  2061.8 138.2 %reduce-scatter.19.cloned.1.call-done = f32[16,2048]{1,0:T(8,128)} async-done(((f32[512,2048]{1,0:T(8,128)}), f32[16,2048]{1,0:T(8,128)}) %reduce-scatter.19.cloned.1.call-update) | async-done | bytes 131088 | tf_op jit(solution)/shard_map/while/body/eval_jaxpr/reduce_scatter | solution.py:257
  2204.9 37.0 all-reduce.5
  2241.9 40.0 all-gather.3
  2282.2 37.2 all_gather.53
  2320.5 42.1 all_gather.54
  2392.3 14.0 fusion.184
  2447.6 14.8 convert_reduce_fusion.15
  2462.3 15.7 multiply_reduce_fusion.20
  2478.1 15.4 multiply_convert_fusion.10
  2547.7 37.0 all-reduce.6
  2588.3 53.2 %reduce-scatter.23.cloned.1.call-done = f32[16,8]{1,0:T(8,128)} async-done(((f32[512,8]{1,0:T(8,128)}), f32[16,8]{1,0:T(8,128)}) %reduce-scatter.23.cloned.1.call-update) | async-done | bytes 528 | tf_op jit(solution)/shard_map/while
  2642.3 130.8 %reduce-scatter.25.cloned.1.call-done = f32[16,20]{1,0:T(8,128)} async-done(((f32[512,20]{1,0:T(8,128)}), f32[16,20]{1,0:T(8,128)}) %reduce-scatter.25.cloned.1.call-update) | async-done | bytes 1296 | tf_op jit(solution)/shard_map/while
  2773.9 132.0 %reduce-scatter.17.cloned.1.call-done = f32[512,16]{0,1:T(8,128)} async-done(((f32[512,512]{0,1:T(8,128)}), f32[512,16]{0,1:T(8,128)}) %reduce-scatter.17.cloned.1.call-update) | async-done | bytes 32784 | tf_op jit(solution)/shard_map/while/body/eval_jaxpr/reduce_scatter | solution.py:256
  2906.7 102.1 %reduce-scatter.15.cloned.1.call-done = f32[16,1536]{1,0:T(8,128)} async-done(((f32[512,1536]{1,0:T(8,128)}), f32[16,1536]{1,0:T(8,128)}) %reduce-scatter.15.cloned.1.call-update) | async-done | bytes 98320 | tf_op jit(solution)/shard_map/while/body/eval_jaxpr/reduce_scatter | solution.py:255
  3009.8 141.3 %reduce-scatter.21.cloned.1.call-done = f32[2048,16]{0,1:T(8,128)} async-done(((f32[2048,512]{0,1:T(8,128)}), f32[2048,16]{0,1:T(8,128)}) %reduce-scatter.21.cloned.1.call-update) | async-done | bytes 131088 | tf_op jit(solution)/shard_map/while/body/eval_jaxpr/reduce_scatter | solution.py:258
  3152.0 138.2 %reduce-scatter.19.cloned.1.call-done = f32[16,2048]{1,0:T(8,128)} async-done(((f32[512,2048]{1,0:T(8,128)}), f32[16,2048]{1,0:T(8,128)}) %reduce-scatter.19.cloned.1.call-update) | async-done | bytes 131088 | tf_op jit(solution)/shard_map/while/body/eval_jaxpr/reduce_scatter | solution.py:257
  3295.1 37.0 all-reduce.5
  3332.1 40.1 all-gather.3
  3372.5 37.3 all_gather.53
  3410.9 42.4 all_gather.54
  3483.0 14.0 fusion.184
  3538.3 14.8 convert_reduce_fusion.15
  3553.1 15.7 multiply_reduce_fusion.20
  3568.8 15.4 multiply_convert_fusion.10
  3620.2 9.8 convolution_bitcast_fusion.11
  3638.4 37.0 all-reduce.6
  3679.0 53.0 %reduce-scatter.23.cloned.1.call-done = f32[16,8]{1,0:T(8,128)} async-done(((f32[512,8]{1,0:T(8,128)}), f32[16,8]{1,0:T(8,128)}) %reduce-scatter.23.cloned.1.call-update) | async-done | bytes 528 | tf_op jit(solution)/shard_map/while
  3732.8 130.9 %reduce-scatter.25.cloned.1.call-done = f32[16,20]{1,0:T(8,128)} async-done(((f32[512,20]{1,0:T(8,128)}), f32[16,20]{1,0:T(8,128)}) %reduce-scatter.25.cloned.1.call-update) | async-done | bytes 1296 | tf_op jit(solution)/shard_map/while
  3864.5 132.0 %reduce-scatter.17.cloned.1.call-done = f32[512,16]{0,1:T(8,128)} async-done(((f32[512,512]{0,1:T(8,128)}), f32[512,16]{0,1:T(8,128)}) %reduce-scatter.17.cloned.1.call-update) | async-done | bytes 32784 | tf_op jit(solution)/shard_map/while/body/eval_jaxpr/reduce_scatter | solution.py:256
  3997.3 102.1 %reduce-scatter.15.cloned.1.call-done = f32[16,1536]{1,0:T(8,128)} async-done(((f32[512,1536]{1,0:T(8,128)}), f32[16,1536]{1,0:T(8,128)}) %reduce-scatter.15.cloned.1.call-update) | async-done | bytes 98320 | tf_op jit(solution)/shard_map/while/body/eval_jaxpr/reduce_scatter | solution.py:255
  4100.3 141.8 %reduce-scatter.21.cloned.1.call-done = f32[2048,16]{0,1:T(8,128)} async-done(((f32[2048,512]{0,1:T(8,128)}), f32[2048,16]{0,1:T(8,128)}) %reduce-scatter.21.cloned.1.call-update) | async-done | bytes 131088 | tf_op jit(solution)/shard_map/while/body/eval_jaxpr/reduce_scatter | solution.py:258
  4243.1 138.5 %reduce-scatter.19.cloned.1.call-done = f32[16,2048]{1,0:T(8,128)} async-done(((f32[512,2048]{1,0:T(8,128)}), f32[16,2048]{1,0:T(8,128)}) %reduce-scatter.19.cloned.1.call-update) | async-done | bytes 131088 | tf_op jit(solution)/shard_map/while/body/eval_jaxpr/reduce_scatter | solution.py:257
  4399.7 36.9 psum.7
  (914 shorter events, 562.0 us)
Async XLA Ops:
  14.6 171.3 %all-gather.8.cloned.1.call-start = ((), (), s32[]{:S(2)}) async-start(), calls=%async_computation.6 | async-start | bytes 1622016 | tf_op jit(solution)/shard_map/while/body/eval_jaxpr/all_gather | solution.py:240
  15.3 211.3 %all-gather.10.cloned.1.call-start = ((), (), s32[]{:S(2)}) async-start(), calls=%async_computation.7 | async-start | bytes 2162688 | tf_op jit(solution)/shard_map/while/body/eval_jaxpr/all_gather | solution.py:242
  16.0 218.2 %all-gather.12.cloned.1.call-start = ((), (), s32[]{:S(2)}) async-start(), calls=%async_computation.8 | async-start | bytes 2162688 | tf_op jit(solution)/shard_map/while/body/eval_jaxpr/all_gather | solution.py:243
  16.8 443.2 %reduce-scatter.23.cloned.1.call-start = ((), (), s32[]{:S(2)}) async-start(), calls=%async_computation.13 | async-start | bytes 270336 | tf_op jit(solution)/shard_map/while
  330.2 261.4 %reduce-scatter.25.cloned.1.call-start = ((), (), s32[]{:S(2)}) async-start(), calls=%async_computation.14 | async-start | bytes 270336 | tf_op jit(solution)/shard_map/while
  337.2 387.1 %reduce-scatter.17.cloned.1.call-start = ((), (), s32[]{:S(2)}) async-start(), calls=%async_computation.10 | async-start | bytes 1081344 | tf_op jit(solution)/shard_map/while/body/eval_jaxpr/reduce_scatter | solution.py:256
  340.4 486.9 %reduce-scatter.15.cloned.1.call-start = ((), (), s32[]{:S(2)}) async-start(), calls=%async_computation.9 | async-start | bytes 3244032 | tf_op jit(solution)/shard_map/while/body/eval_jaxpr/reduce_scatter | solution.py:255
  347.1 622.9 %reduce-scatter.21.cloned.1.call-start = ((), (), s32[]{:S(2)}) async-start(), calls=%async_computation.12 | async-start | bytes 4325376 | tf_op jit(solution)/shard_map/while/body/eval_jaxpr/reduce_scatter | solution.py:258
  358.1 751.7 %reduce-scatter.19.cloned.1.call-start = ((), (), s32[]{:S(2)}) async-start(), calls=%async_computation.11 | async-start | bytes 4325376 | tf_op jit(solution)/shard_map/while/body/eval_jaxpr/reduce_scatter | solution.py:257
  405.5 704.3 %copy-start.23 = (f32[16,2048]{1,0:T(8,128)S(1)}, f32[16,2048]{1,0:T(8,128)}, u32[]{:S(2)}) copy-start(f32[16,2048]{1,0:T(8,128)} %get-tuple-element.930) | copy-start | bytes 393220 | tf_op jit(solution)/shard_map/while
  405.5 705.9 %copy-start.35 = (bf16[16,1536]{1,0:T(8,128)(2,1)S(1)}, bf16[16,1536]{1,0:T(8,128)(2,1)}, u32[]{:S(2)}) copy-start(bf16[16,1536]{1,0:T(8,128)(2,1)} %copy-done.34) | copy-start | bytes 147460 | tf_op jit(solution)/shard_map/while
  405.5 705.9 %copy-start.43 = (bf16[512,16]{0,1:T(8,128)(2,1)S(1)}, bf16[512,16]{0,1:T(8,128)(2,1)}, u32[]{:S(2)}) copy-start(bf16[512,16]{0,1:T(8,128)(2,1)} %copy-done.42) | copy-start | bytes 49156 | tf_op jit(solution)/shard_map/while
  405.6 705.9 %copy-start.54 = (bf16[20,16]{0,1:T(8,128)(2,1)S(1)}, bf16[20,16]{0,1:T(8,128)(2,1)}, u32[]{:S(2)}) copy-start(bf16[20,16]{0,1:T(8,128)(2,1)} %copy-done.53) | copy-start | bytes 1924 | tf_op jit(solution)/shard_map/while
  405.6 705.9 %copy-start.58 = (pred[532]{0:T(1024)(128)(4,1)S(1)}, pred[532]{0:T(1024)(128)(4,1)}, u32[]{:S(2)}) copy-start(pred[532]{0:T(1024)(128)(4,1)} %copy-done.57) | copy-start | bytes 1600 | tf_op jit(solution)/shard_map/while
  405.6 705.9 %copy-start.60 = (bf16[8,16]{1,0:T(8,128)(2,1)S(1)}, bf16[8,16]{1,0:T(8,128)(2,1)}, u32[]{:S(2)}) copy-start(bf16[8,16]{1,0:T(8,128)(2,1)} %copy-done.59) | copy-start | bytes 772 | tf_op jit(solution)/shard_map/while
  460.8 650.0 %copy-start.52 = (f32[8,16]{1,0:T(8,128)}, f32[8,16]{1,0:T(8,128)S(1)}, u32[]{:S(2)}) copy-start(f32[8,16]{1,0:T(8,128)S(1)} %select_add_fusion.16) | copy-start | bytes 1540 | tf_op jit(solution)/shard_map/while
  1111.7 165.6 %all-gather.8.cloned.1.call-start = ((), (), s32[]{:S(2)}) async-start(), calls=%async_computation.6 | async-start | bytes 1622016 | tf_op jit(solution)/shard_map/while/body/eval_jaxpr/all_gather | solution.py:240
  1112.3 205.7 %all-gather.10.cloned.1.call-start = ((), (), s32[]{:S(2)}) async-start(), calls=%async_computation.7 | async-start | bytes 2162688 | tf_op jit(solution)/shard_map/while/body/eval_jaxpr/all_gather | solution.py:242
  1113.0 212.6 %all-gather.12.cloned.1.call-start = ((), (), s32[]{:S(2)}) async-start(), calls=%async_computation.8 | async-start | bytes 2162688 | tf_op jit(solution)/shard_map/while/body/eval_jaxpr/all_gather | solution.py:243
  1113.6 437.9 %reduce-scatter.23.cloned.1.call-start = ((), (), s32[]{:S(2)}) async-start(), calls=%async_computation.13 | async-start | bytes 270336 | tf_op jit(solution)/shard_map/while
  1421.5 261.6 %reduce-scatter.25.cloned.1.call-start = ((), (), s32[]{:S(2)}) async-start(), calls=%async_computation.14 | async-start | bytes 270336 | tf_op jit(solution)/shard_map/while
  1428.5 387.3 %reduce-scatter.17.cloned.1.call-start = ((), (), s32[]{:S(2)}) async-start(), calls=%async_computation.10 | async-start | bytes 1081344 | tf_op jit(solution)/shard_map/while/body/eval_jaxpr/reduce_scatter | solution.py:256
  1431.7 486.9 %reduce-scatter.15.cloned.1.call-start = ((), (), s32[]{:S(2)}) async-start(), calls=%async_computation.9 | async-start | bytes 3244032 | tf_op jit(solution)/shard_map/while/body/eval_jaxpr/reduce_scatter | solution.py:255
  1438.3 622.5 %reduce-scatter.21.cloned.1.call-start = ((), (), s32[]{:S(2)}) async-start(), calls=%async_computation.12 | async-start | bytes 4325376 | tf_op jit(solution)/shard_map/while/body/eval_jaxpr/reduce_scatter | solution.py:258
  1449.4 750.6 %reduce-scatter.19.cloned.1.call-start = ((), (), s32[]{:S(2)}) async-start(), calls=%async_computation.11 | async-start | bytes 4325376 | tf_op jit(solution)/shard_map/while/body/eval_jaxpr/reduce_scatter | solution.py:257
  1496.7 703.3 %copy-start.23 = (f32[16,2048]{1,0:T(8,128)S(1)}, f32[16,2048]{1,0:T(8,128)}, u32[]{:S(2)}) copy-start(f32[16,2048]{1,0:T(8,128)} %get-tuple-element.930) | copy-start | bytes 393220 | tf_op jit(solution)/shard_map/while
  1496.7 704.9 %copy-start.35 = (bf16[16,1536]{1,0:T(8,128)(2,1)S(1)}, bf16[16,1536]{1,0:T(8,128)(2,1)}, u32[]{:S(2)}) copy-start(bf16[16,1536]{1,0:T(8,128)(2,1)} %copy-done.34) | copy-start | bytes 147460 | tf_op jit(solution)/shard_map/while
  1496.7 704.9 %copy-start.43 = (bf16[512,16]{0,1:T(8,128)(2,1)S(1)}, bf16[512,16]{0,1:T(8,128)(2,1)}, u32[]{:S(2)}) copy-start(bf16[512,16]{0,1:T(8,128)(2,1)} %copy-done.42) | copy-start | bytes 49156 | tf_op jit(solution)/shard_map/while
  1496.7 704.9 %copy-start.54 = (bf16[20,16]{0,1:T(8,128)(2,1)S(1)}, bf16[20,16]{0,1:T(8,128)(2,1)}, u32[]{:S(2)}) copy-start(bf16[20,16]{0,1:T(8,128)(2,1)} %copy-done.53) | copy-start | bytes 1924 | tf_op jit(solution)/shard_map/while
  1496.7 704.9 %copy-start.58 = (pred[532]{0:T(1024)(128)(4,1)S(1)}, pred[532]{0:T(1024)(128)(4,1)}, u32[]{:S(2)}) copy-start(pred[532]{0:T(1024)(128)(4,1)} %copy-done.57) | copy-start | bytes 1600 | tf_op jit(solution)/shard_map/while
  1496.8 704.9 %copy-start.60 = (bf16[8,16]{1,0:T(8,128)(2,1)S(1)}, bf16[8,16]{1,0:T(8,128)(2,1)}, u32[]{:S(2)}) copy-start(bf16[8,16]{1,0:T(8,128)(2,1)} %copy-done.59) | copy-start | bytes 772 | tf_op jit(solution)/shard_map/while
  1552.2 648.7 %copy-start.52 = (f32[8,16]{1,0:T(8,128)}, f32[8,16]{1,0:T(8,128)S(1)}, u32[]{:S(2)}) copy-start(f32[8,16]{1,0:T(8,128)S(1)} %select_add_fusion.16) | copy-start | bytes 1540 | tf_op jit(solution)/shard_map/while
  2201.9 165.3 %all-gather.8.cloned.1.call-start = ((), (), s32[]{:S(2)}) async-start(), calls=%async_computation.6 | async-start | bytes 1622016 | tf_op jit(solution)/shard_map/while/body/eval_jaxpr/all_gather | solution.py:240
  2202.6 205.3 %all-gather.10.cloned.1.call-start = ((), (), s32[]{:S(2)}) async-start(), calls=%async_computation.7 | async-start | bytes 2162688 | tf_op jit(solution)/shard_map/while/body/eval_jaxpr/all_gather | solution.py:242
  2203.2 212.4 %all-gather.12.cloned.1.call-start = ((), (), s32[]{:S(2)}) async-start(), calls=%async_computation.8 | async-start | bytes 2162688 | tf_op jit(solution)/shard_map/while/body/eval_jaxpr/all_gather | solution.py:243
  2203.9 437.5 %reduce-scatter.23.cloned.1.call-start = ((), (), s32[]{:S(2)}) async-start(), calls=%async_computation.13 | async-start | bytes 270336 | tf_op jit(solution)/shard_map/while
  2511.4 261.7 %reduce-scatter.25.cloned.1.call-start = ((), (), s32[]{:S(2)}) async-start(), calls=%async_computation.14 | async-start | bytes 270336 | tf_op jit(solution)/shard_map/while
  2518.4 387.5 %reduce-scatter.17.cloned.1.call-start = ((), (), s32[]{:S(2)}) async-start(), calls=%async_computation.10 | async-start | bytes 1081344 | tf_op jit(solution)/shard_map/while/body/eval_jaxpr/reduce_scatter | solution.py:256
  2521.6 487.2 %reduce-scatter.15.cloned.1.call-start = ((), (), s32[]{:S(2)}) async-start(), calls=%async_computation.9 | async-start | bytes 3244032 | tf_op jit(solution)/shard_map/while/body/eval_jaxpr/reduce_scatter | solution.py:255
  2528.3 622.8 %reduce-scatter.21.cloned.1.call-start = ((), (), s32[]{:S(2)}) async-start(), calls=%async_computation.12 | async-start | bytes 4325376 | tf_op jit(solution)/shard_map/while/body/eval_jaxpr/reduce_scatter | solution.py:258
  2539.3 750.9 %reduce-scatter.19.cloned.1.call-start = ((), (), s32[]{:S(2)}) async-start(), calls=%async_computation.11 | async-start | bytes 4325376 | tf_op jit(solution)/shard_map/while/body/eval_jaxpr/reduce_scatter | solution.py:257
  2586.6 703.6 %copy-start.23 = (f32[16,2048]{1,0:T(8,128)S(1)}, f32[16,2048]{1,0:T(8,128)}, u32[]{:S(2)}) copy-start(f32[16,2048]{1,0:T(8,128)} %get-tuple-element.930) | copy-start | bytes 393220 | tf_op jit(solution)/shard_map/while
  2586.6 705.2 %copy-start.35 = (bf16[16,1536]{1,0:T(8,128)(2,1)S(1)}, bf16[16,1536]{1,0:T(8,128)(2,1)}, u32[]{:S(2)}) copy-start(bf16[16,1536]{1,0:T(8,128)(2,1)} %copy-done.34) | copy-start | bytes 147460 | tf_op jit(solution)/shard_map/while
  2586.6 705.2 %copy-start.43 = (bf16[512,16]{0,1:T(8,128)(2,1)S(1)}, bf16[512,16]{0,1:T(8,128)(2,1)}, u32[]{:S(2)}) copy-start(bf16[512,16]{0,1:T(8,128)(2,1)} %copy-done.42) | copy-start | bytes 49156 | tf_op jit(solution)/shard_map/while
  2586.7 705.2 %copy-start.54 = (bf16[20,16]{0,1:T(8,128)(2,1)S(1)}, bf16[20,16]{0,1:T(8,128)(2,1)}, u32[]{:S(2)}) copy-start(bf16[20,16]{0,1:T(8,128)(2,1)} %copy-done.53) | copy-start | bytes 1924 | tf_op jit(solution)/shard_map/while
  2586.7 705.2 %copy-start.58 = (pred[532]{0:T(1024)(128)(4,1)S(1)}, pred[532]{0:T(1024)(128)(4,1)}, u32[]{:S(2)}) copy-start(pred[532]{0:T(1024)(128)(4,1)} %copy-done.57) | copy-start | bytes 1600 | tf_op jit(solution)/shard_map/while
  2586.7 705.2 %copy-start.60 = (bf16[8,16]{1,0:T(8,128)(2,1)S(1)}, bf16[8,16]{1,0:T(8,128)(2,1)}, u32[]{:S(2)}) copy-start(bf16[8,16]{1,0:T(8,128)(2,1)} %copy-done.59) | copy-start | bytes 772 | tf_op jit(solution)/shard_map/while
  2642.3 648.9 %copy-start.52 = (f32[8,16]{1,0:T(8,128)}, f32[8,16]{1,0:T(8,128)S(1)}, u32[]{:S(2)}) copy-start(f32[8,16]{1,0:T(8,128)S(1)} %select_add_fusion.16) | copy-start | bytes 1540 | tf_op jit(solution)/shard_map/while
  3292.1 165.8 %all-gather.8.cloned.1.call-start = ((), (), s32[]{:S(2)}) async-start(), calls=%async_computation.6 | async-start | bytes 1622016 | tf_op jit(solution)/shard_map/while/body/eval_jaxpr/all_gather | solution.py:240
  3292.8 205.9 %all-gather.10.cloned.1.call-start = ((), (), s32[]{:S(2)}) async-start(), calls=%async_computation.7 | async-start | bytes 2162688 | tf_op jit(solution)/shard_map/while/body/eval_jaxpr/all_gather | solution.py:242
  3293.6 212.8 %all-gather.12.cloned.1.call-start = ((), (), s32[]{:S(2)}) async-start(), calls=%async_computation.8 | async-start | bytes 2162688 | tf_op jit(solution)/shard_map/while/body/eval_jaxpr/all_gather | solution.py:243
  3294.2 437.9 %reduce-scatter.23.cloned.1.call-start = ((), (), s32[]{:S(2)}) async-start(), calls=%async_computation.13 | async-start | bytes 270336 | tf_op jit(solution)/shard_map/while
  3602.1 261.6 %reduce-scatter.25.cloned.1.call-start = ((), (), s32[]{:S(2)}) async-start(), calls=%async_computation.14 | async-start | bytes 270336 | tf_op jit(solution)/shard_map/while
  3609.2 387.3 %reduce-scatter.17.cloned.1.call-start = ((), (), s32[]{:S(2)}) async-start(), calls=%async_computation.10 | async-start | bytes 1081344 | tf_op jit(solution)/shard_map/while/body/eval_jaxpr/reduce_scatter | solution.py:256
  3612.3 487.0 %reduce-scatter.15.cloned.1.call-start = ((), (), s32[]{:S(2)}) async-start(), calls=%async_computation.9 | async-start | bytes 3244032 | tf_op jit(solution)/shard_map/while/body/eval_jaxpr/reduce_scatter | solution.py:255
  3619.0 623.1 %reduce-scatter.21.cloned.1.call-start = ((), (), s32[]{:S(2)}) async-start(), calls=%async_computation.12 | async-start | bytes 4325376 | tf_op jit(solution)/shard_map/while/body/eval_jaxpr/reduce_scatter | solution.py:258
  3630.1 751.5 %reduce-scatter.19.cloned.1.call-start = ((), (), s32[]{:S(2)}) async-start(), calls=%async_computation.11 | async-start | bytes 4325376 | tf_op jit(solution)/shard_map/while/body/eval_jaxpr/reduce_scatter | solution.py:257
  3677.4 704.1 %copy-start.23 = (f32[16,2048]{1,0:T(8,128)S(1)}, f32[16,2048]{1,0:T(8,128)}, u32[]{:S(2)}) copy-start(f32[16,2048]{1,0:T(8,128)} %get-tuple-element.930) | copy-start | bytes 393220 | tf_op jit(solution)/shard_map/while
  3677.4 705.7 %copy-start.35 = (bf16[16,1536]{1,0:T(8,128)(2,1)S(1)}, bf16[16,1536]{1,0:T(8,128)(2,1)}, u32[]{:S(2)}) copy-start(bf16[16,1536]{1,0:T(8,128)(2,1)} %copy-done.34) | copy-start | bytes 147460 | tf_op jit(solution)/shard_map/while
  3677.4 705.7 %copy-start.43 = (bf16[512,16]{0,1:T(8,128)(2,1)S(1)}, bf16[512,16]{0,1:T(8,128)(2,1)}, u32[]{:S(2)}) copy-start(bf16[512,16]{0,1:T(8,128)(2,1)} %copy-done.42) | copy-start | bytes 49156 | tf_op jit(solution)/shard_map/while
  3677.4 705.7 %copy-start.54 = (bf16[20,16]{0,1:T(8,128)(2,1)S(1)}, bf16[20,16]{0,1:T(8,128)(2,1)}, u32[]{:S(2)}) copy-start(bf16[20,16]{0,1:T(8,128)(2,1)} %copy-done.53) | copy-start | bytes 1924 | tf_op jit(solution)/shard_map/while
  3677.4 705.7 %copy-start.58 = (pred[532]{0:T(1024)(128)(4,1)S(1)}, pred[532]{0:T(1024)(128)(4,1)}, u32[]{:S(2)}) copy-start(pred[532]{0:T(1024)(128)(4,1)} %copy-done.57) | copy-start | bytes 1600 | tf_op jit(solution)/shard_map/while
  3677.4 705.7 %copy-start.60 = (bf16[8,16]{1,0:T(8,128)(2,1)S(1)}, bf16[8,16]{1,0:T(8,128)(2,1)}, u32[]{:S(2)}) copy-start(bf16[8,16]{1,0:T(8,128)(2,1)} %copy-done.59) | copy-start | bytes 772 | tf_op jit(solution)/shard_map/while
  3732.8 649.7 %copy-start.52 = (f32[8,16]{1,0:T(8,128)}, f32[8,16]{1,0:T(8,128)S(1)}, u32[]{:S(2)}) copy-start(f32[8,16]{1,0:T(8,128)S(1)} %select_add_fusion.16) | copy-start | bytes 1540 | tf_op jit(solution)/shard_map/while
  (232 other events, 18194.8 us)
Sparse Core Ops, SparseCore 0:
  18.9 57.8 all-gather.7
  80.1 55.3 all-gather.9
  139.0 55.4 all-gather.11
  330.3 129.6 reduce-scatter.22
  462.1 129.3 reduce-scatter.24
  593.6 130.6 reduce-scatter.16
  729.8 97.4 reduce-scatter.14
  829.6 140.2 reduce-scatter.20
  972.3 137.4 reduce-scatter.18
  1115.7 51.0 all-gather.7
  1170.2 55.4 all-gather.9
  1229.0 55.5 all-gather.11
  1421.6 129.8 reduce-scatter.22
  1553.6 129.4 reduce-scatter.24
  1685.1 130.6 reduce-scatter.16
  1821.1 97.4 reduce-scatter.14
  1920.8 139.9 reduce-scatter.20
  2063.1 136.8 reduce-scatter.18
  2206.2 51.0 all-gather.7
  2260.5 55.4 all-gather.9
  2319.4 55.4 all-gather.11
  2511.5 129.9 reduce-scatter.22
  2643.7 129.3 reduce-scatter.24
  2775.2 130.6 reduce-scatter.16
  2911.4 97.4 reduce-scatter.14
  3011.1 139.9 reduce-scatter.20
  3153.3 136.8 reduce-scatter.18
  3296.4 51.0 all-gather.7
  3350.9 55.4 all-gather.9
  3409.7 55.5 all-gather.11
  3602.2 129.7 reduce-scatter.22
  3734.3 129.3 reduce-scatter.24
  3865.8 130.6 reduce-scatter.16
  4001.9 97.4 reduce-scatter.14
  4101.8 140.3 reduce-scatter.20
  4244.3 137.1 reduce-scatter.18
where the time goes:
time: 4460 us
  waiting for transfers between devices  2800 us (63%)
  blocking collectives  817 us (18%)
  matrix products  503 us (11%)
  other arithmetic  166 us (4%)
  local copies, waits for them, and re-layouts  143 us (3%)
    while x44, waiting for transfers between devices  741 us
    reduce_scatter x4, waiting for transfers between devices, micro_step(): lax.psum_scatter(grads[3], ('dp', 'fsdp'), scatter_dimension=1, tiled=True)  566 us
    reduce_scatter x4, waiting for transfers between devices, micro_step(): lax.psum_scatter(grads[2], ('dp', 'fsdp'), scatter_dimension=0, tiled=True)  554 us
    reduce_scatter x4, waiting for transfers between devices, micro_step(): lax.psum_scatter(grads[1], ('dp', 'fsdp'), scatter_dimension=1, tiled=True)  528 us
    reduce_scatter x4, waiting for transfers between devices, micro_step(): lax.psum_scatter(grads[0], ('dp', 'fsdp'), scatter_dimension=0, tiled=True)  408 us
    while x8, blocking collectives  301 us
    all_gather x4, blocking collectives, micro_step(): lax.all_gather(lowered[1], ('dp', 'fsdp'), axis=1, tiled=True)  169 us
    all_gather x4, blocking collectives, micro_step(): lax.all_gather(lowered[4], ('dp', 'fsdp'), axis=1, tiled=True)  160 us
  transfers between devices with their start and end apart: 36, of which 24 were waited for; matrix products, arithmetic and copies ran while one was open for 8% of the time, Pallas kernels for 0%

commit v1 on v0

v1 whole, which is shorter than its diff:
```python
from functools import partial

import jax
import jax.numpy as jnp
from jax import lax
from jax.experimental import pallas as pl
from jax.experimental.pallas import tpu as pltpu
from jax.sharding import PartitionSpec as P

STEP = 7
HDIM = 64
PAD = 32
HALF = 256
FCHUNK = 256
ROWS = 32
BF = jnp.bfloat16
FL = jnp.float32
AXES = ("dp", "fsdp")
NEG = -1e30
EPS = 1e-05
SCALE = HDIM ** (-0.5)


def dot(a, b, ca, cb):
    return lax.dot_general(a, b, (((ca,), (cb,)), ((), ())), preferred_element_type=FL)


def head_mask(rows, width):
    row = lax.broadcasted_iota(jnp.int32, (rows, width), 0) // PAD
    col = lax.broadcasted_iota(jnp.int32, (rows, width), 1) // HDIM
    return row == col


def spread(x, heads):
    tiled = jnp.concatenate([x.astype(FL)] * heads, axis=0)
    return jnp.where(head_mask(*tiled.shape), tiled, 0.0).astype(BF)


def fold(y, heads):
    own = jnp.where(head_mask(*y.shape), y, 0.0)
    return sum(own[h * PAD : (h + 1) * PAD] for h in range(heads))


def pair_masks(width):
    col = lax.broadcasted_iota(jnp.int32, (1, width), 1)
    low = jnp.where(col < HDIM, 1.0, 0.0)
    return low.astype(BF), (1.0 - low).astype(BF)


def attend_kernel(
    extra,
    tok_ref,
    state_ref,
    memb_ref,
    vec_ref,
    inw_ref,
    qkv_ref,
    pt_ref,
    ptk_ref,
    ptq_ref,
    mixed_ref,
    vt_ref,
    sk_ref,
    ot_ref,
):
    length, width = tok_ref.shape[1:]
    heads = width // HDIM
    rows = length + PAD
    memory = (state_ref[0].astype(FL) + memb_ref[...]).astype(BF)
    inputs = jnp.concatenate([tok_ref[0], memory], axis=0)
    qkv_ref[0, :, :width] = ((dot(inputs, inw_ref[:, :width], 1, 0) + vec_ref[0:1, :]) * SCALE).astype(BF)
    qkv_ref[0, :, width : 2 * width] = dot(inputs, inw_ref[:, width : 2 * width], 1, 0).astype(BF)
    qkv_ref[0, :, 2 * width :] = (dot(inputs, inw_ref[:, 2 * width :], 1, 0) + vec_ref[1:2, :]).astype(BF)
    vt_ref[...] = qkv_ref[0, :length, 2 * width :].T

    key_place = lax.broadcasted_iota(jnp.int32, (heads * PAD, 1), 0) % PAD
    k_mem = spread(qkv_ref[0, length:, width : 2 * width], heads)
    sk_ref[...] = jnp.where(key_place < extra, dot(k_mem, qkv_ref[0, :length, :width], 1, 1), NEG)

    q_mem = spread(qkv_ref[0, length:, :width], heads)
    sq = dot(qkv_ref[0, :, width : 2 * width], q_mem, 1, 1)
    place = lax.broadcasted_iota(jnp.int32, (rows, 1), 0)
    sq = jnp.where(place < length + extra, sq, NEG)
    eq = jnp.exp(sq - jnp.max(sq, axis=0, keepdims=True))
    ptq_ref[0] = (eq * (1.0 / jnp.sum(eq, axis=0, keepdims=True))).astype(BF)
    om = dot(ptq_ref[0], qkv_ref[0, :, 2 * width :], 0, 0)
    mixed_ref[0, length:, :] = fold(om, heads).astype(BF)

    diag = lax.broadcasted_iota(jnp.int32, (HALF, HALF), 0) <= lax.broadcasted_iota(
        jnp.int32, (HALF, HALF), 1
    )
    masks = pair_masks(2 * HDIM)

    def pair(p, carry):
        lanes = pl.ds(pl.multiple_of(p * 2 * HDIM, 2 * HDIM), 2 * HDIM)
        key_lanes = pl.ds(pl.multiple_of(width + p * 2 * HDIM, 2 * HDIM), 2 * HDIM)
        kp = qkv_ref[0, :length, key_lanes]
        for side in range(2):
            h = 2 * p + side
            km = kp * masks[side]
            own = pl.ds(pl.multiple_of(h * PAD, PAD), PAD)
            feat = pl.ds(pl.multiple_of(h * HDIM, HDIM), HDIM)
            for part in range(length // HALF):
                cols = pl.ds(part * HALF, HALF)
                below = part * HALF
                upto = below + HALF
                qp = qkv_ref[0, cols, lanes]
                s_diag = jnp.where(diag, dot(km[below:upto], qp, 1, 1), NEG)
                s_mem = sk_ref[own, cols]
                top = jnp.maximum(
                    jnp.max(s_diag, axis=0, keepdims=True), jnp.max(s_mem, axis=0, keepdims=True)
                )
                if part:
                    s_low = dot(km[:below], qp, 1, 1)
                    top = jnp.maximum(top, jnp.max(s_low, axis=0, keepdims=True))
                e_diag = jnp.exp(s_diag - top)
                e_mem = jnp.exp(s_mem - top)
                total = jnp.sum(e_diag, axis=0, keepdims=True) + jnp.sum(e_mem, axis=0, keepdims=True)
                if part:
                    e_low = jnp.exp(s_low - top)
                    total = total + jnp.sum(e_low, axis=0, keepdims=True)
                share = 1.0 / total
                base = part * (part + 1) // 2 * HALF
                if part:
                    pt_ref[0, h, base : base + below, :] = (e_low * share).astype(BF)
                pt_ref[0, h, base + below : base + upto, :] = (e_diag * share).astype(BF)
                ptk_ref[0, own, cols] = (e_mem * share).astype(BF)
                ot_ref[feat, cols] = dot(vt_ref[feat, :upto], pt_ref[0, h, base : base + upto, :], 1, 0)
        return carry

    lax.fori_loop(0, heads // 2, pair, 0)
    v_mem = spread(qkv_ref[0, length:, 2 * width :], heads)
    om_t = ot_ref[...] + dot(v_mem, ptk_ref[0], 0, 0)
    mixed_ref[0, :length, :] = om_t.astype(BF).T


def attend(extra, tok, state, memb, vecs, in_w):
    count, length, width = tok.shape
    heads = width // HDIM
    rows = length + PAD
    parts = length // HALF
    ptrows = parts * (parts + 1) // 2 * HALF
    one = lambda *dims: pl.BlockSpec((1,) + dims, lambda b: (b,) + (0,) * len(dims))
    whole = lambda *dims: pl.BlockSpec(dims, lambda b: (0,) * len(dims))
    return pl.pallas_call(
        partial(attend_kernel, extra),
        grid=(count,),
        in_specs=[
            one(length, width),
            one(PAD, width),
            whole(PAD, width),
            whole(8, width),
            whole(width, 3 * width),
        ],
        out_specs=[
            one(rows, 3 * width),
            one(heads, ptrows, HALF),
            one(heads * PAD, length),
            one(rows, heads * PAD),
            one(rows, width),
        ],
        out_shape=[
            jax.ShapeDtypeStruct((count, rows, 3 * width), BF),
            jax.ShapeDtypeStruct((count, heads, ptrows, HALF), BF),
            jax.ShapeDtypeStruct((count, heads * PAD, length), BF),
            jax.ShapeDtypeStruct((count, rows, heads * PAD), BF),
            jax.ShapeDtypeStruct((count, rows, width), BF),
        ],
        scratch_shapes=[
            pltpu.VMEM((width, length), BF),
            pltpu.VMEM((heads * PAD, length), FL),
            pltpu.VMEM((width, length), FL),
        ],
        compiler_params=pltpu.CompilerParams(vmem_limit_bytes=56 << 20),
        name="attend",
    )(tok, state, memb, vecs, in_w)


def norm_rows(x):
    center = x - jnp.mean(x, axis=-1, keepdims=True)
    rstd = lax.rsqrt(jnp.mean(center * center, axis=-1, keepdims=True) + EPS)
    return center * rstd, rstd


def norm_back(grad, normed, rstd, gain):
    scaled = grad * gain
    return rstd * (
        scaled
        - jnp.mean(scaled, axis=-1, keepdims=True)
        - normed * jnp.mean(scaled * normed, axis=-1, keepdims=True)
    )


def by_eight(x):
    return jnp.sum(x.reshape(x.shape[0] // 8, 8, x.shape[1]), axis=0)


def feed_kernel(
    tok_ref,
    state_ref,
    memb_ref,
    vec_ref,
    upb_ref,
    wide_ref,
    mixed_ref,
    cot_ref,
    out_ref,
    one_ref,
    gm_ref,
    gwide_ref,
    gvec_ref,
    gupb_ref,
    acc_ref,
    sums_ref,
    upb_sum_ref,
    att_ref,
    n1_ref,
    r1_ref,
    low_ref,
    g2_ref,
    gb_ref,
    hidden_ref,
    slope_ref,
    gpre_ref,
    ga_ref,
    m_low_ref,
    m_gb_ref,
    m_ga_ref,
    m_mixed_ref,
    m_hidden_ref,
    m_gpre_ref,
):
    step = pl.program_id(0)
    last = pl.num_programs(0) - 1
    length, width = tok_ref.shape[1:]
    hid = upb_ref.shape[1]
    rows = length + PAD
    up = slice(0, hid)
    down = slice(hid, 2 * hid)
    outw = slice(2 * hid, 2 * hid + width)

    @pl.when(step == 0)
    def _():
        acc_ref[...] = jnp.zeros_like(acc_ref)
        sums_ref[...] = jnp.zeros_like(sums_ref)
        upb_sum_ref[...] = jnp.zeros_like(upb_sum_ref)

    att_ref[...] = dot(mixed_ref[0], wide_ref[:, outw], 1, 1)
    att_ref[:length] += tok_ref[0].astype(FL)
    att_ref[length:] += state_ref[0].astype(FL) + memb_ref[...]
    bias_att, bias_ffn = vec_ref[2:3, :], vec_ref[3:4, :]
    gain_one, shift_one, gain_two, shift_two = (vec_ref[i : i + 1, :] for i in range(4, 8))

    def norm_one(i, carry):
        r = pl.ds(pl.multiple_of(i * ROWS, ROWS), ROWS)
        normed, rstd = norm_rows(att_ref[r, :] + bias_att)
        n1_ref[r, :] = normed
        r1_ref[r, :] = rstd
        low_ref[r, :] = (normed * gain_one + shift_one).astype(BF)
        return carry

    lax.fori_loop(0, rows // ROWS, norm_one, 0, unroll=True)

    root = 0.7978845608
    for j in range(0, hid, FCHUNK):
        c = slice(j, j + FCHUNK)
        v = dot(low_ref[...], wide_ref[:, c], 1, 0) + upb_ref[:, c]
        square = v * v
        half = 0.5 + 0.5 * jnp.tanh(v * (root + (root * 0.044715) * square))
        act = v * half
        hidden_ref[:, c] = act.astype(BF)
        slope_ref[:, c] = half + (act * (1.0 - half)) * (2 * root + (6 * root * 0.044715) * square)

    att_ref[...] = dot(hidden_ref[...], wide_ref[:, down], 1, 1)

    def norm_two(i, carry):
        r = pl.ds(pl.multiple_of(i * ROWS, ROWS), ROWS)
        first = n1_ref[r, :] * gain_one + shift_one
        normed, rstd = norm_rows(first + (att_ref[r, :] + bias_ffn))
        out_ref[0, r, :] = (normed * gain_two + shift_two).astype(BF)
        cot = cot_ref[0, r, :].astype(FL)
        sums_ref[48:56] += by_eight(cot * normed)
        sums_ref[56:64] += by_eight(cot)
        back = norm_back(cot, normed, rstd, gain_two)
        g2_ref[r, :] = back
        low = back.astype(BF)
        gb_ref[r, :] = low
        sums_ref[24:32] += by_eight(low.astype(FL))
        return carry

    lax.fori_loop(0, rows // ROWS, norm_two, 0, unroll=True)

    for j in range(0, hid, FCHUNK):
        c = slice(j, j + FCHUNK)
        d = slice(hid + j, hid + j + FCHUNK)
        gpre = (dot(gb_ref[...], wide_ref[:, d], 1, 0) * slope_ref[:, c]).astype(BF)
        gpre_ref[:, c] = gpre
        upb_sum_ref[:, c] += by_eight(gpre.astype(FL))
        acc_ref[:, d] += dot(gb_ref[:length], hidden_ref[:length, c], 0, 0)
        acc_ref[:, c] += dot(low_ref[:length], gpre_ref[:length, c], 0, 0)

    att_ref[...] = dot(gpre_ref[...], wide_ref[:, up], 1, 1)

    def norm_last(i, carry):
        r = pl.ds(pl.multiple_of(i * ROWS, ROWS), ROWS)
        g1 = g2_ref[r, :] + att_ref[r, :]
        normed = n1_ref[r, :]
        sums_ref[32:40] += by_eight(g1 * normed)
        sums_ref[40:48] += by_eight(g1)
        back = norm_back(g1, normed, r1_ref[r, :], gain_one)
        one_ref[0, r, :] = back
        low = back.astype(BF)
        ga_ref[r, :] = low
        sums_ref[16:24] += by_eight(low.astype(FL))
        return carry

    lax.fori_loop(0, rows // ROWS, norm_last, 0, unroll=True)

    gm_ref[0] = dot(ga_ref[...], wide_ref[:, outw], 1, 0).astype(BF)
    acc_ref[:, outw] += dot(ga_ref[:length], mixed_ref[0, :length], 0, 0)

    mem = pl.ds(pl.multiple_of(step * PAD, PAD), PAD)
    m_low_ref[mem, :] = low_ref[length:, :]
    m_gb_ref[mem, :] = gb_ref[length:, :]
    m_ga_ref[mem, :] = ga_ref[length:, :]
    m_mixed_ref[mem, :] = mixed_ref[0, length:, :]
    m_hidden_ref[mem, :] = hidden_ref[length:, :]
    m_gpre_ref[mem, :] = gpre_ref[length:, :]

    @pl.when(step == last)
    def _():
        for j in range(0, hid, FCHUNK):
            c = slice(j, j + FCHUNK)
            d = slice(hid + j, hid + j + FCHUNK)
            gwide_ref[:, c] = (acc_ref[:, c] + dot(m_low_ref[...], m_gpre_ref[:, c], 0, 0)).astype(BF)
            gwide_ref[:, d] = (acc_ref[:, d] + dot(m_gb_ref[...], m_hidden_ref[:, c], 0, 0)).astype(BF)
        gwide_ref[:, outw] = (acc_ref[:, outw] + dot(m_ga_ref[...], m_mixed_ref[...], 0, 0)).astype(BF)
        for i in range(8):
            gvec_ref[i : i + 1, :] = jnp.sum(sums_ref[8 * i : 8 * i + 8], axis=0, keepdims=True)
        gupb_ref[...] = jnp.sum(upb_sum_ref[...], axis=0, keepdims=True)


def feed(tok, state, memb, vecs, upb, wide, mixed, cot):
    count, length, width = tok.shape
    rows = length + PAD
    hid = upb.shape[1]
    cols = wide.shape[1]
    one = lambda *dims: pl.BlockSpec((1,) + dims, lambda b: (b,) + (0,) * len(dims))
    whole = lambda *dims: pl.BlockSpec(dims, lambda b: (0,) * len(dims), pipeline_mode=pl.Buffered(1))
    final = lambda *dims: pl.BlockSpec(dims, lambda b: (0,) * len(dims))
    vm = pltpu.VMEM
    return pl.pallas_call(
        feed_kernel,
        grid=(count,),
        in_specs=[
            one(length, width),
            one(PAD, width),
            whole(PAD, width),
            whole(8, width),
            whole(1, hid),
            whole(width, cols),
            one(rows, width),
            one(rows, width),
        ],
        out_specs=[
            one(rows, width),
            one(rows, width),
            one(rows, width),
            final(width, cols),
            final(8, width),
            final(1, hid),
        ],
        out_shape=[
            jax.ShapeDtypeStruct((count, rows, width), BF),
            jax.ShapeDtypeStruct((count, rows, width), FL),
            jax.ShapeDtypeStruct((count, rows, width), BF),
            jax.ShapeDtypeStruct((width, cols), BF),
            jax.ShapeDtypeStruct((8, width), FL),
            jax.ShapeDtypeStruct((1, hid), FL),
        ],
        scratch_shapes=[
            vm((width, cols), FL),
            vm((64, width), FL),
            vm((8, hid), FL),
            vm((rows, width), FL),
            vm((rows, width), FL),
            vm((rows, 1), FL),
            vm((rows, width), BF),
            vm((rows, width), FL),
            vm((rows, width), BF),
            vm((rows, hid), BF),
            vm((rows, hid), FL),
            vm((rows, hid), BF),
            vm((rows, width), BF),
            vm((count * PAD, width), BF),
            vm((count * PAD, width), BF),
            vm((count * PAD, width), BF),
            vm((count * PAD, width), BF),
            vm((count * PAD, hid), BF),
            vm((count * PAD, hid), BF),
        ],
        compiler_params=pltpu.CompilerParams(vmem_limit_bytes=60 << 20),
        name="feed",
    )(tok, state, memb, vecs, upb, wide, mixed, cot)


def return_kernel(
    tok_ref,
    state_ref,
    memb_ref,
    inw_ref,
    qkv_ref,
    pt_ref,
    ptk_ref,
    ptq_ref,
    gm_ref,
    one_ref,
    grad_ref,
    gin_ref,
    acc_ref,
    sums_ref,
    kt_ref,
    dpk_ref,
    dsk_ref,
    dqt_ref,
    dk_ref,
    dv_ref,
    dj_ref,
    m_in_ref,
    m_dj_ref,
    side_ref,
):
    step = pl.program_id(0)
    last = pl.num_programs(0) - 1
    length, width = tok_ref.shape[1:]
    heads = width // HDIM

    @pl.when(step == 0)
    def _():
        acc_ref[...] = jnp.zeros_like(acc_ref)
        sums_ref[...] = jnp.zeros_like(sums_ref)
        side_ref[...] = jnp.zeros_like(side_ref)

    kt_ref[...] = qkv_ref[0, :length, width : 2 * width].T
    q_mem = spread(qkv_ref[0, length:, :width], heads)
    k_mem = spread(qkv_ref[0, length:, width : 2 * width], heads)
    v_mem = spread(qkv_ref[0, length:, 2 * width :], heads)
    do_mem = spread(gm_ref[0, length:, :], heads)

    dpk_ref[...] = dot(v_mem, gm_ref[0, :length, :], 1, 1)
    dpq = dot(qkv_ref[0, :, 2 * width :], do_mem, 1, 1)
    pq = ptq_ref[0].astype(FL)
    tq = pq * dpq
    dsq = (tq - pq * jnp.sum(tq, axis=0, keepdims=True)).astype(BF)
    dv_ref[...] = dot(ptq_ref[0], do_mem, 1, 0)
    dk_ref[...] = dot(dsq, q_mem, 1, 0)
    dj_ref[length:, :width] = (fold(dot(dsq, qkv_ref[0, :, width : 2 * width], 0, 0), heads) * SCALE).astype(BF)

    masks = pair_masks(2 * HDIM)

    def pair(p, carry):
        lanes = pl.ds(pl.multiple_of(p * 2 * HDIM, 2 * HDIM), 2 * HDIM)
        key_lanes = pl.ds(pl.multiple_of(width + p * 2 * HDIM, 2 * HDIM), 2 * HDIM)
        val_lanes = pl.ds(pl.multiple_of(2 * width + p * 2 * HDIM, 2 * HDIM), 2 * HDIM)
        vp = qkv_ref[0, :length, val_lanes]
        dop = gm_ref[0, :length, lanes]
        qp = qkv_ref[0, :length, lanes]
        for side in range(2):
            h = 2 * p + side
            own = pl.ds(pl.multiple_of(h * PAD, PAD), PAD)
            feat = pl.ds(pl.multiple_of(h * HDIM, HDIM), HDIM)
            vm = vp * masks[side]
            dom = dop * masks[side]
            qm = qp * masks[side]
            for part in range(length // HALF):
                cols = slice(part * HALF, (part + 1) * HALF)
                upto = (part + 1) * HALF
                base = part * (part + 1) // 2 * HALF
                block = slice(base, base + upto)
                dp = dot(vm[:upto], dop[cols], 1, 1)
                prob = pt_ref[0, h, block, :]
                pf = prob.astype(FL)
                t = pf * dp
                pm = ptk_ref[0, own, cols].astype(FL)
                tm = pm * dpk_ref[own, cols]
                delta = jnp.sum(t, axis=0, keepdims=True) + jnp.sum(tm, axis=0, keepdims=True)
                ds = (t - pf * delta).astype(BF)
                dsk_ref[own, cols] = (tm - pm * delta).astype(BF)
                dv_ref[:upto, lanes] += dot(prob, dom[cols], 1, 0)
                dk_ref[:upto, lanes] += dot(ds, qm[cols], 1, 0)
                dqt_ref[feat, cols] = dot(kt_ref[feat, :upto], ds, 1, 0)
        return carry

    lax.fori_loop(0, heads // 2, pair, 0)

    dq_t = dqt_ref[...] + dot(k_mem, dsk_ref[...], 0, 0)
    dj_ref[:length, :width] = (dq_t * SCALE).astype(BF).T
    dv_ref[length:, :] += fold(dot(ptk_ref[0], gm_ref[0, :length, :], 1, 0), heads)
    dk_ref[length:, :] += fold(dot(dsk_ref[...], qkv_ref[0, :length, :width], 1, 0), heads)
    dj_ref[:, width : 2 * width] = dk_ref[...].astype(BF)
    dj_ref[:, 2 * width :] = dv_ref[...].astype(BF)
    sums_ref[0:8] += by_eight(dj_ref[:, :width].astype(FL))
    sums_ref[8:16] += by_eight(dj_ref[:, 2 * width :].astype(FL))

    mem = pl.ds(pl.multiple_of(step * PAD, PAD), PAD)
    m_in_ref[mem, :] = (state_ref[0].astype(FL) + memb_ref[...]).astype(BF)
    m_dj_ref[mem, :] = dj_ref[length:, :]
    for j in range(3):
        c = slice(j * width, (j + 1) * width)
        acc_ref[:, c] += dot(tok_ref[0], dj_ref[:length, c], 0, 0)
    grad_ref[0] = one_ref[0, :length, :] + dot(dj_ref[:length, :], inw_ref[...], 1, 1)
    side_ref[0:PAD, :] += one_ref[0, length:, :] + dot(dj_ref[length:, :], inw_ref[...], 1, 1)

    @pl.when(step == last)
    def _():
        for j in range(3):
            c = slice(j * width, (j + 1) * width)
            gin_ref[:, c] = (acc_ref[:, c] + dot(m_in_ref[...], m_dj_ref[:, c], 0, 0)).astype(BF)
        side_ref[PAD : PAD + 1, :] = jnp.sum(sums_ref[0:8], axis=0, keepdims=True)
        side_ref[PAD + 1 : PAD + 2, :] = jnp.sum(sums_ref[8:16], axis=0, keepdims=True)
        gin_ref[:, 3 * width :] = side_ref[...].T.astype(BF)


def go_back(tok, state, memb, in_w, qkv, pt, ptk, ptq, gm, one_grad):
    count, length, width = tok.shape
    rows = length + PAD
    heads = width // HDIM
    one = lambda *dims: pl.BlockSpec((1,) + dims, lambda b: (b,) + (0,) * len(dims))
    whole = lambda *dims: pl.BlockSpec(dims, lambda b: (0,) * len(dims), pipeline_mode=pl.Buffered(1))
    final = lambda *dims: pl.BlockSpec(dims, lambda b: (0,) * len(dims))
    vm = pltpu.VMEM
    return pl.pallas_call(
        return_kernel,
        grid=(count,),
        in_specs=[
            one(length, width),
            one(PAD, width),
            whole(PAD, width),
            whole(width, 3 * width),
            one(rows, 3 * width),
            one(*pt.shape[1:]),
            one(heads * PAD, length),
            one(rows, heads * PAD),
            one(rows, width),
            one(rows, width),
        ],
        out_specs=[one(length, width), final(width, 3 * width + 128)],
        out_shape=[
            jax.ShapeDtypeStruct((count, length, width), FL),
            jax.ShapeDtypeStruct((width, 3 * width + 128), BF),
        ],
        scratch_shapes=[
            vm((width, 3 * width), FL),
            vm((16, width), FL),
            vm((width, length), BF),
            vm((heads * PAD, length), FL),
            vm((heads * PAD, length), BF),
            vm((width, length), FL),
            vm((rows, width), FL),
            vm((rows, width), FL),
            vm((rows, 3 * width), BF),
            vm((count * PAD, width), BF),
            vm((count * PAD, 3 * width), BF),
            vm((128, width), FL),
        ],
        compiler_params=pltpu.CompilerParams(vmem_limit_bytes=60 << 20),
        name="go_back",
    )(tok, state, memb, in_w, qkv, pt, ptk, ptq, gm, one_grad)


def gather(x, devices, index):
    rows, cols = x.shape
    held = x[None]
    bit = devices // 2
    while bit:
        got = lax.ppermute(held, AXES, [(i, i ^ bit) for i in range(devices)])
        upper = (index & bit) != 0
        held = jnp.stack([jnp.where(upper, got, held), jnp.where(upper, held, got)], axis=1)
        held = held.reshape(-1, rows, cols)
        bit //= 2
    return held.reshape(devices * rows, cols)


def scatter_sum(x, devices, index):
    total, cols = x.shape
    rows = total // devices
    held = x
    bit = 1
    while bit < devices:
        held = held.reshape(-1, 2, rows, cols)
        upper = (index & bit) != 0
        keep = jnp.where(upper, held[:, 1], held[:, 0]).astype(FL)
        send = jnp.where(upper, held[:, 0], held[:, 1]).astype(BF)
        held = keep + lax.ppermute(send, AXES, [(i, i ^ bit) for i in range(devices)]).astype(FL)
        bit *= 2
    return held.reshape(rows, cols)


def butterfly(x, devices):
    bit = 1
    while bit < devices:
        x = x + lax.ppermute(x, AXES, [(i, i ^ bit) for i in range(devices)])
        bit *= 2
    return x


def adam_step(weight, first, second, grad, rate, decay):
    first_new = 0.5 * first + 0.5 * grad
    second_new = 0.5 * second + 0.5 * grad * grad
    correction = 1.0 - 0.5**STEP
    weight_new = weight - rate * (
        first_new / correction / (jnp.sqrt(second_new / correction) + 1e-08) + decay * weight
    )
    return (weight_new, first_new, second_new)


def per_device(
    devices,
    tokens,
    memory_state,
    cotangent,
    in_weight,
    in_first,
    in_second,
    out_weight,
    out_first,
    out_second,
    up_weight,
    up_first,
    up_second,
    down_weight,
    down_first,
    down_second,
    vectors,
    vectors_first,
    vectors_second,
    up_bias,
    up_bias_first,
    up_bias_second,
    memory_embed,
    memory_first,
    memory_second,
):
    index = lax.axis_index(AXES)
    micro, local, length, width = tokens.shape
    count = micro * local
    extra = memory_state.shape[2]
    shard = in_weight.shape[0]
    hid = up_weight.shape[1]
    per_bias = up_bias.shape[0] // shard

    small = jnp.concatenate(
        [
            memory_embed.T,
            jnp.zeros((shard, PAD - extra), FL),
            vectors.T,
            up_bias.reshape(per_bias, shard).T,
            jnp.zeros((shard, 128 - PAD - 8 - per_bias), FL),
        ],
        axis=1,
    )
    near = jnp.concatenate([in_weight, small], axis=1).astype(BF)
    far = jnp.concatenate([up_weight, down_weight.T, out_weight.T], axis=1).astype(BF)
    near = gather(near, devices, index)
    wide = gather(far, devices, index)
    side = near[:, 3 * width :].astype(FL).T
    memb = side[:PAD]
    vecs = side[PAD : PAD + 8]
    upb = side[PAD + 8 : PAD + 8 + per_bias].reshape(per_bias, devices, shard)
    upb = upb.transpose(1, 0, 2).reshape(1, hid)
    in_w = near[:, : 3 * width]

    tok = tokens.reshape(count, length, width)
    state = jnp.pad(memory_state.reshape(count, extra, width), ((0, 0), (0, PAD - extra), (0, 0)))
    cot = cotangent.reshape(count, extra + length, width)
    cot = jnp.concatenate(
        [cot[:, extra:], cot[:, :extra], jnp.zeros((count, PAD - extra, width), BF)], axis=1
    )

    qkv, pt, ptk, ptq, mixed = attend(extra, tok, state, memb, vecs, in_w)
    out, one_grad, gm, gwide, gvec, gupb = feed(tok, state, memb, vecs, upb, wide, mixed, cot)
    gupb = gupb.reshape(devices, per_bias, shard).transpose(1, 0, 2).reshape(per_bias, width)
    gside = jnp.concatenate(
        [jnp.zeros((PAD, width), FL), gvec, gupb, jnp.zeros((128 - PAD - 8 - per_bias, width), FL)]
    ).T.astype(BF)
    gfar = scatter_sum(jnp.concatenate([gwide, gside], axis=1), devices, index)
    input_grad, gnear = go_back(tok, state, memb, in_w, qkv, pt, ptk, ptq, gm, one_grad)
    gnear = scatter_sum(gnear, devices, index)

    output = jnp.concatenate([out[:, length : length + extra], out[:, :length]], axis=1)
    output = output.reshape(micro, local, extra + length, width)
    input_grad = input_grad.reshape(micro, local, length, width)

    gsmall = (gnear[:, 3 * width :] + gfar[:, 2 * hid + width :]).T
    grads = (
        gnear[:, : 3 * width],
        gfar[:, 2 * hid : 2 * hid + width],
        gfar[:, :hid],
        gfar[:, hid : 2 * hid],
        gsmall[PAD : PAD + 8],
        gsmall[PAD + 8 : PAD + 8 + per_bias].reshape(up_bias.shape),
        gsmall[:extra],
    )
    squares = sum(jnp.sum(grad * grad) for grad in grads)
    grad_norm = jnp.sqrt(butterfly(squares.reshape(1, 1), devices)[0, 0])
    factor = 1.0 / jnp.maximum(grad_norm, 1.0)
    total_rows = extra + length
    rates = (
        0.5 * width ** (-0.5),
        0.5 * (width * 32 // total_rows) ** (-0.5),
        0.5 * width ** (-0.5),
        0.5 * hid ** (-0.5),
        0.1,
        0.1,
        0.5,
    )
    decays = (0.1, 0.1, 0.1, 0.1, 0.0, 0.0, 0.0)
    states = (
        (in_weight, in_first, in_second),
        (out_weight.T, out_first.T, out_second.T),
        (up_weight, up_first, up_second),
        (down_weight.T, down_first.T, down_second.T),
        (vectors, vectors_first, vectors_second),
        (up_bias, up_bias_first, up_bias_second),
        (memory_embed, memory_first, memory_second),
    )
    results = []
    for i, (weight, first, second) in enumerate(states):
        new = adam_step(weight, first, second, grads[i] * factor, rates[i], decays[i])
        results.extend(value.T if i in (1, 3) else value for value in new)
    return (output, input_grad, *results, grad_norm)


def solution(mesh):
    blocks = P(None, AXES, None, None)
    lead = P(AXES, None)
    trail = P(None, AXES)
    flat = P(AXES)
    weights = (lead,) * 3 + (trail,) * 3 + (lead,) * 3 + (trail,) * 6 + (flat,) * 3 + (trail,) * 3
    devices = mesh.shape["dp"] * mesh.shape["fsdp"]
    return jax.shard_map(
        partial(per_device, devices),
        mesh=mesh,
        in_specs=(blocks,) * 3 + weights,
        out_specs=(blocks,) * 2 + weights + (P(),),
        check_vma=False,
    )
```

time: 4460 us -> 576 us (0.13)
  waiting for transfers between devices: 2800 us -> 98.4 us
  blocking collectives: 817 us -> 0 us
  matrix products: 503 us -> 0 us
  Pallas kernels: 0 us -> 248 us
  other arithmetic: 166 us -> 72.2 us
    reduce_scatter x16 -> x0, waiting for transfers between devices: 2060 us -> none  [the longest x4 566 us: micro_step(): lax.psum_scatter(grads[3], ('dp', 'fsdp'), scatter_dimension=1, tiled=True)]
    while x44 -> x0, waiting for transfers between devices: 741 us -> none
    dot_general x72 -> x0, matrix products: 503 us -> none  [the longest x4 62.9 us: backward(): jnp.einsum('cqhe,ckhe->chqk', grad_mixed, value_heads, preferred_element_...]
    all_gather x12 -> x0, blocking collectives: 478 us -> none  [the longest x4 169 us: micro_step(): lax.all_gather(lowered[1], ('dp', 'fsdp'), axis=1, tiled=True)]
    while x8 -> x0, blocking collectives: 301 us -> none
    pallas_call x0 -> x3, Pallas kernels: none -> 248 us  [the longest x1 89.9 us: feed(): pl.pallas_call(feed_kernel, grid=(count,), in_specs=[one(length, width),...]
    ppermute x0 -> x25, waiting for transfers between devices: none -> 98.4 us  [the longest x10 52.3 us: gather(): got = lax.ppermute(held, AXES, [(i, i ^ bit) for i in range(devices)])]
    convert_element_type x27 -> x9, other arithmetic: 81.6 us -> 8.99 us  [the longest x8 8.85 us: scatter_sum(): send = jnp.where(upper, held[:, 0], held[:, 1]).astype(BF)]
  transfers between devices with their start and end apart: 36 -> 25, of which waited for: 24 -> 16; matrix products, arithmetic and copies ran while one was open for 8% -> 15% of each run, Pallas kernels for 0% -> 12%
where the time goes in v1:
time: 576 us; the launch traced here: 570 us
  Pallas kernels  248 us (43%)
  local copies, waits for them, and re-layouts  103 us (18%)
  waiting for transfers between devices  98.4 us (17%)
  other arithmetic  72.2 us (13%)
  starting transfers between devices  37.7 us (7%)
  between operations  10.6 us (2%)
    pallas_call x1, Pallas kernels, feed(): pl.pallas_call(feed_kernel, grid=(count,), in_specs=[one(length, width),...  89.9 us
    pallas_call x1, Pallas kernels, go_back(): pl.pallas_call(return_kernel, grid=(count,), in_specs=[one(length, width)...  88.4 us
    pallas_call x1, Pallas kernels, attend(): pl.pallas_call(partial(attend_kernel, extra), grid=(count,), in_specs=[on...  69.3 us
    unnamed x109, local copies, waits for them, and re-layouts  56.3 us
    ppermute x10, waiting for transfers between devices, gather(): got = lax.ppermute(held, AXES, [(i, i ^ bit) for i in range(devices)])  52.3 us
    ppermute x10, waiting for transfers between devices, scatter_sum(): lax.ppermute(send, AXES, [(i, i ^ bit) for i in range(devices)]).astype(FL)  39.6 us
    ppermute x10, starting transfers between devices, scatter_sum(): lax.ppermute(send, AXES, [(i, i ^ bit) for i in range(devices)]).astype(FL)  15.2 us
    ppermute x10, starting transfers between devices, gather(): got = lax.ppermute(held, AXES, [(i, i ^ bit) for i in range(devices)])  11.9 us
  transfers between devices with their start and end apart: 25, of which 16 were waited for; matrix products, arithmetic and copies ran while one was open for 15% of the time, Pallas kernels for 12%

profile of v1, /device:TPU:0, one launch (start us, length us, event | category | flops | bytes accessed | tf_op | source)
XLA Modules:
  0.0 569.7 jit_solution(10468500652613646932)
XLA Ops:
  4.7 4.1 collective-permute-start
  12.7 8.0 %collective-permute-done.5 = bf16[1,16,4608]{2,1,0:T(8,128)(2,1)S(1)} collective-permute-done((bf16[1,16,4608]{2,1,0:T(8,128)(2,1)S(1)}, bf16[1,16,4608]{2,1,0:T(8,128)(2,1)S(1)}, u32[]{:S(2)}, u32[]{:S(2)}) %collective-permute-start.5) | collective-permute-done | bytes 147488 | tf_op jit(solution)/shard_map/ppermute | solution.py:576
  21.0 2.1 collective-permute-start.1
  23.0 6.9 %collective-permute-done.6 = bf16[2,16,4608]{2,1,0:T(8,128)(2,1)S(1)} collective-permute-done((bf16[2,16,4608]{2,1,0:T(8,128)(2,1)S(1)}, bf16[2,16,4608]{2,1,0:T(8,128)(2,1)S(1)}, u32[]{:S(2)}, u32[]{:S(2)}) %collective-permute-start.6) | collective-permute-done | bytes 294944 | tf_op jit(solution)/shard_map/ppermute | solution.py:576
  32.3 9.9 %collective-permute-done.7 = bf16[4,16,4608]{2,1,0:T(8,128)(2,1)S(1)} collective-permute-done((bf16[4,16,4608]{2,1,0:T(8,128)(2,1)S(1)}, bf16[4,16,4608]{2,1,0:T(8,128)(2,1)S(1)}, u32[]{:S(2)}, u32[]{:S(2)}) %collective-permute-start.7) | collective-permute-done | bytes 589856 | tf_op jit(solution)/shard_map/ppermute | solution.py:576
  42.5 2.2 collective-permute-start.8
  47.0 3.7 collective-permute-done.2
  51.0 20.0 %collective-permute-done.8 = bf16[8,16,4608]{2,1,0:T(8,128)(2,1)S(1)} collective-permute-done((bf16[8,16,4608]{2,1,0:T(8,128)(2,1)S(1)}, bf16[8,16,4608]{2,1,0:T(8,128)(2,1)S(1)}, u32[]{:S(2)}, u32[]{:S(2)}) %collective-permute-start.8) | collective-permute-done | bytes 1179680 | tf_op jit(solution)/shard_map/ppermute | solution.py:576
  71.7 3.8 collective-permute-done.3
  77.3 3.1 slice.177
  82.6 2.1 copy.396
  90.3 2.2 copy.406
  92.6 2.3 copy.402
  96.2 2.3 copy.409
  98.5 2.2 copy.411
  102.3 5.8 %maximum_maximum_fusion.cot_ref = bf16[8,544,512]{2,1,0:T(8,128)(2,1)} fusion(bf16[8,20,512]{2,1,0:T(8,128)(2,1)S(1)} %slice.178, bf16[8,512,512]{2,1,0:T(8,128)(2,1)} %slice.177, bf16[544]{0:T(1024)(128)(2,1)S(1)} %pad.15.clone), kind=kLoop, calls=%fused_computation.6 | loop fusion | flops 13369344 | bytes 8815680 | tf_op jit(solution)/shard_map/concatenate | solution.py:676
  113.7 69.3 %attend.1 = (bf16[8,544,1536]{2,1,0:T(8,128)(2,1)}, bf16[8,8,768,256]{3,2,1,0:T(8,128)(2,1)}, bf16[8,256,512]{2,1,0:T(8,128)(2,1)}, bf16[8,544,256]{2,1,0:T(8,128)(2,1)}, bf16[8,544,512]{2,1,0:T(8,128)(2,1)}) custom-call(bf16[8,512,512]{2,1,0:T(8,128)(2,1)} %bitcast.337, bf16[8,32,512]{2,1,0:T(8,128)(2,1)} %pad.4.state_ref, f32[32,512]{1,0:T(8,128)} %copy.355.memb_ref, ...), custom_call_target="tpu_custom_call" | custom-call | tf_op jit(solution)/shard_map/attend/pallas_call | solution.py:145
  183.0 2.0 select_bitcast_fusion.2
  185.4 2.5 copy.351
  187.9 89.9 %feed.1 = (bf16[8,544,512]{2,1,0:T(8,128)(2,1)}, f32[8,544,512]{2,1,0:T(8,128)}, bf16[8,544,512]{2,1,0:T(8,128)(2,1)}, bf16[512,4608]{1,0:T(8,128)(2,1)}, f32[8,512]{1,0:T(8,128)}, /*index=5*/f32[1,2048]{1,0:T(1,128)}) custom-call(bf16[8,512,512]{2,1,0:T(8,128)(2,1)} %bitcast.338, bf16[8,32,512]{2,1,0:T(8,128)(2,1)} %pad.4.state_ref, ...), custom_call_target="tpu_custom_call" | custom-call | tf_op jit(solution)/shard_map/feed/pallas_call | solution.py:352
  279.8 88.4 %go_back.1 = (f32[8,512,512]{2,1,0:T(8,128)}, bf16[512,1664]{1,0:T(8,128)(2,1)}) custom-call(bf16[8,512,512]{2,1,0:T(8,128)(2,1)} %bitcast.339, bf16[8,32,512]{2,1,0:T(8,128)(2,1)} %pad.4.state_ref, f32[32,512]{1,0:T(8,128)} %copy.355.memb_ref, bf16[512,1536]{1,0:T(8,128)(2,1)} %slice.176.inw_ref, bf16[8,544,1536]{2,1,0:T(8,128)(2,1)} %get-tuple-element.39.qkv_ref, ...), custom_call_target="tpu_custom_call" | custom-call | tf_op jit(solution)/shard_map/go_back/pallas_call | solution.py:532
  370.4 2.7 pad_maximum_fusion
  373.4 2.0 copy-done
  378.5 9.6 %collective-permute-done.11 = bf16[8,16,1664]{2,1,0:T(8,128)(2,1)S(1)} collective-permute-done((bf16[8,16,1664]{2,1,0:T(8,128)(2,1)S(1)}, bf16[8,16,1664]{2,1,0:T(8,128)(2,1)S(1)}, u32[]{:S(2)}, u32[]{:S(2)}) %collective-permute-start.11) | collective-permute-done | bytes 426016 | tf_op jit(solution)/shard_map/ppermute | solution.py:594
  393.6 2.1 copy.393
  395.7 4.6 slice.142
  403.0 2.6 convert_add_fusion
  405.6 2.2 copy-done.1
  411.8 1.6 copy.437
  414.7 2.1 copy.371
  417.6 3.3 pad_maximum_fusion.2
  420.9 5.4 copy.416
  426.7 10.2 %collective-permute-done.16 = bf16[8,16,4736]{2,1,0:T(8,128)(2,1)} collective-permute-done((bf16[8,16,4736]{2,1,0:T(8,128)(2,1)}, bf16[8,16,4736]{2,1,0:T(8,128)(2,1)}, u32[]{:S(2)}, u32[]{:S(2)}) %collective-permute-start.16) | collective-permute-done | bytes 1212448 | tf_op jit(solution)/shard_map/ppermute | solution.py:594
  436.9 3.2 fusion.3
  441.9 12.0 %collective-permute-done.17 = bf16[4,16,4736]{2,1,0:T(8,128)(2,1)S(1)} collective-permute-done((bf16[4,16,4736]{2,1,0:T(8,128)(2,1)S(1)}, bf16[4,16,4736]{2,1,0:T(8,128)(2,1)S(1)}, u32[]{:S(2)}, u32[]{:S(2)}) %collective-permute-start.17) | collective-permute-done | bytes 606240 | tf_op jit(solution)/shard_map/ppermute | solution.py:594
  454.1 3.0 copy.442
  457.1 3.2 copy.443
  460.3 4.3 fusion.1
  464.6 2.1 copy.387
  468.5 4.5 collective-permute-start.14
  473.0 5.4 collective-permute-done.18
  478.4 2.7 copy.388
  481.1 4.5 fusion
  485.6 2.2 copy-done.2
  488.4 3.2 collective-permute-start.19
  491.5 2.5 collective-permute-done.14
  495.9 1.8 copy.390
  497.7 3.5 fusion.4
  512.0 2.9 collective-permute-start.21
  516.4 1.9 collective-permute-start.22
  518.3 1.8 collective-permute-done.22
  522.3 2.1 collective-permute-done.23
  525.1 3.2 collective-permute-start.24
  536.0 6.2 %fusion.31 = (f32[2048,16]{1,0:T(8,128)}, f32[2048,16]{1,0:T(8,128)}, f32[2048,16]{1,0:T(8,128)}, f32[16,2048]{0,1:T(8,128)}, f32[16,2048]{0,1:T(8,128)}, /*index=5*/f32[16,2048]{0,1:T(8,128)}) fusion(f32[]{:T(128)S(6)} %div.66, f32[16,4736]{0,1:T(8,128)S(1)} %fusion.4, f32[2048,16]{1,0:T(8,128)} %copy.411, f32[2048,16]{1,0:T(8,128)} %copy.409, ...), kind=kLoop, calls=%fused_computation.103 | loop fusion | flops 819200 | bytes 1966084 | tf_op jit(solution)/shard_map/transpose | solution.py:730
  542.2 2.3 copy.423
  544.5 2.2 copy.424
  546.7 2.2 copy.425
  549.8 2.3 copy.427
  552.1 2.2 copy.428
  554.3 2.1 fusion.36
  556.4 1.7 copy.420
  558.0 1.7 copy.421
  559.7 1.7 copy.422
  561.4 2.4 multiply_subtract_fusion.1
  (231 shorter events, 81.3 us)
Async XLA Ops:
  0.7 9.7 %copy-start.25 = (f32[512,16]{0,1:T(8,128)S(1)}, f32[512,16]{0,1:T(8,128)}, u32[]{:S(2)}) copy-start(f32[512,16]{0,1:T(8,128)} %param.30) | copy-start | bytes 98308
  0.7 9.9 %copy-start.15 = (f32[16,2048]{1,0:T(8,128)S(1)}, f32[16,2048]{1,0:T(8,128)}, u32[]{:S(2)}) copy-start(f32[16,2048]{1,0:T(8,128)} %param.33) | copy-start | bytes 393220
  4.7 6.7 %copy-start.19 = (f32[16,2048]{1,0:T(8,128)S(1)}, f32[16,2048]{1,0:T(8,128)}, u32[]{:S(2)}) copy-start(f32[16,2048]{1,0:T(8,128)} %param.34) | copy-start | bytes 393220
  4.7 7.3 %copy-start.20 = (f32[16,2048]{1,0:T(8,128)S(1)}, f32[16,2048]{1,0:T(8,128)}, u32[]{:S(2)}) copy-start(f32[16,2048]{1,0:T(8,128)} %param.35) | copy-start | bytes 393220
  4.7 16.2 %collective-permute-start = (bf16[1,16,1664]{2,1,0:T(8,128)(2,1)S(1)}, bf16[1,16,1664]{2,1,0:T(8,128)(2,1)S(1)}, u32[]{:S(2)}, u32[]{:S(2)}) collective-permute-start(bf16[1,16,1664]{2,1,0:T(8,128)(2,1)S(1)} %concatenate.53), channel_id=1, source_target_pairs={{0,16},{1,17},{2,18},{3,19},{4,20},{5,21},{6,22},{7,23},{8,24},{9,... | collective-permute-start | bytes 159752 | tf_op jit(solution)/shard_map/ppermute | solution.py:576
  10.1 10.7 %copy-start.7 = (f32[2048,16]{1,0:T(8,128)}, f32[2048,16]{1,0:T(8,128)S(1)}, u32[]{:S(2)}) copy-start(f32[2048,16]{1,0:T(8,128)S(1)} %copy.343) | copy-start | bytes 393220
  10.5 19.5 %copy-start.13 = (f32[512,16]{1,0:T(8,128)}, f32[512,16]{1,0:T(8,128)S(1)}, u32[]{:S(2)}) copy-start(f32[512,16]{1,0:T(8,128)S(1)} %copy.344) | copy-start | bytes 98308
  11.3 20.3 %copy-start.21 = (f32[2048,16]{0,1:T(8,128)S(1)}, f32[2048,16]{0,1:T(8,128)}, u32[]{:S(2)}) copy-start(f32[2048,16]{0,1:T(8,128)} %param.37) | copy-start | bytes 393220
  11.3 9.4 %collective-permute-start.5 = (bf16[1,16,4608]{2,1,0:T(8,128)(2,1)S(1)}, bf16[1,16,4608]{2,1,0:T(8,128)(2,1)S(1)}, u32[]{:S(2)}, u32[]{:S(2)}) collective-permute-start(bf16[1,16,4608]{2,1,0:T(8,128)(2,1)S(1)} %pad_maximum_fusion.10), channel_id=1, source_target_pairs={{0,16},{1,17},{2,18},{3,19},{4,20},{5,21},{6,22},{7,23},{8,24},{9,... | collective-permute-start | bytes 442376 | tf_op jit(solution)/shard_map/ppermute | solution.py:576
  20.8 9.1 %collective-permute-start.6 = (bf16[2,16,4608]{2,1,0:T(8,128)(2,1)S(1)}, bf16[2,16,4608]{2,1,0:T(8,128)(2,1)S(1)}, u32[]{:S(2)}, u32[]{:S(2)}) collective-permute-start(bf16[2,16,4608]{2,1,0:T(8,128)(2,1)S(1)} %maximum_bitcast_fusion), channel_id=1, source_target_pairs={{0,8},{1,9},{2,10},{3,11},{4,12},{5,13},{6,14},{7,15},{8,0},{9,1},... | collective-permute-start | bytes 884744 | tf_op jit(solution)/shard_map/ppermute | solution.py:576
  21.0 11.3 %collective-permute-start.1 = (bf16[2,16,1664]{2,1,0:T(8,128)(2,1)S(1)}, bf16[2,16,1664]{2,1,0:T(8,128)(2,1)S(1)}, u32[]{:S(2)}, u32[]{:S(2)}) collective-permute-start(bf16[2,16,1664]{2,1,0:T(8,128)(2,1)S(1)} %maximum_bitcast_fusion.2), channel_id=1, source_target_pairs={{0,8},{1,9},{2,10},{3,11},{4,12},{5,13},{6,14},{7,15},{8,0},{9,1},... | collective-permute-start | bytes 319496 | tf_op jit(solution)/shard_map/ppermute | solution.py:576
  30.0 12.2 %collective-permute-start.7 = (bf16[4,16,4608]{2,1,0:T(8,128)(2,1)S(1)}, bf16[4,16,4608]{2,1,0:T(8,128)(2,1)S(1)}, u32[]{:S(2)}, u32[]{:S(2)}) collective-permute-start(bf16[4,16,4608]{2,1,0:T(8,128)(2,1)S(1)} %bitcast.363), channel_id=1, source_target_pairs={{0,4},{1,5},{2,6},{3,7},{4,0},{5,1},{6,2},{7,3},{8,12},{9,13},{10,... | collective-permute-start | bytes 1769480 | tf_op jit(solution)/shard_map/ppermute | solution.py:576
  42.3 4.0 copy-start.22
  42.5 28.5 %collective-permute-start.8 = (bf16[8,16,4608]{2,1,0:T(8,128)(2,1)S(1)}, bf16[8,16,4608]{2,1,0:T(8,128)(2,1)S(1)}, u32[]{:S(2)}, u32[]{:S(2)}) collective-permute-start(bf16[8,16,4608]{2,1,0:T(8,128)(2,1)S(1)} %bitcast.358), channel_id=1, source_target_pairs={{0,2},{1,3},{2,0},{3,1},{4,6},{5,7},{6,4},{7,5},{8,10},{9,11},{10,... | collective-permute-start | bytes 3538952 | tf_op jit(solution)/shard_map/ppermute | solution.py:576
  44.8 5.9 %collective-permute-start.2 = (bf16[4,16,1664]{2,1,0:T(8,128)(2,1)S(1)}, bf16[4,16,1664]{2,1,0:T(8,128)(2,1)S(1)}, u32[]{:S(2)}, u32[]{:S(2)}) collective-permute-start(bf16[4,16,1664]{2,1,0:T(8,128)(2,1)S(1)} %bitcast.367), channel_id=1, source_target_pairs={{0,4},{1,5},{2,6},{3,7},{4,0},{5,1},{6,2},{7,3},{8,12},{9,13},{10,... | collective-permute-start | bytes 638984 | tf_op jit(solution)/shard_map/ppermute | solution.py:576
  50.9 24.7 %collective-permute-start.3 = (bf16[8,16,1664]{2,1,0:T(8,128)(2,1)S(1)}, bf16[8,16,1664]{2,1,0:T(8,128)(2,1)S(1)}, u32[]{:S(2)}, u32[]{:S(2)}) collective-permute-start(bf16[8,16,1664]{2,1,0:T(8,128)(2,1)S(1)} %bitcast.364), channel_id=1, source_target_pairs={{0,2},{1,3},{2,0},{3,1},{4,6},{5,7},{6,4},{7,5},{8,10},{9,11},{10,... | collective-permute-start | bytes 1277960 | tf_op jit(solution)/shard_map/ppermute | solution.py:576
  71.2 5.3 slice-start.2
  71.5 5.1 slice-start.3
  71.7 4.3 copy-start.26
  71.7 111.3 %collective-permute-start.9 = (bf16[16,16,4608]{2,1,0:T(8,128)(2,1)S(1)}, bf16[16,16,4608]{2,1,0:T(8,128)(2,1)}, u32[]{:S(2)}, u32[]{:S(2)}) collective-permute-start(bf16[16,16,4608]{2,1,0:T(8,128)(2,1)S(1)} %bitcast.350), channel_id=1, source_target_pairs={{0,1},{1,0},{2,3},{3,2},{4,5},{5,4},{6,7},{7,6},{8,9},{9,8},{10,11... | collective-permute-start | bytes 7077896 | tf_op jit(solution)/shard_map/ppermute | solution.py:576
  75.8 32.2 %collective-permute-start.4 = (bf16[16,16,1664]{2,1,0:T(8,128)(2,1)S(1)}, bf16[16,16,1664]{2,1,0:T(8,128)(2,1)}, u32[]{:S(2)}, u32[]{:S(2)}) collective-permute-start(bf16[16,16,1664]{2,1,0:T(8,128)(2,1)S(1)} %bitcast.362), channel_id=1, source_target_pairs={{0,1},{1,0},{2,3},{3,2},{4,5},{5,4},{6,7},{7,6},{8,9},{9,8},{10,11... | collective-permute-start | bytes 2555912 | tf_op jit(solution)/shard_map/ppermute | solution.py:576
  82.6 12.2 %copy-start.16 = (f32[16,2048]{1,0:T(8,128)S(1)}, f32[16,2048]{1,0:T(8,128)}, u32[]{:S(2)}) copy-start(f32[16,2048]{1,0:T(8,128)} %broadcast_multiply_fusion.3) | copy-start | bytes 393220
  102.3 5.8 %copy-start.23 = (f32[16,1536]{1,0:T(8,128)S(1)}, f32[16,1536]{1,0:T(8,128)}, u32[]{:S(2)}) copy-start(f32[16,1536]{1,0:T(8,128)} %param.28) | copy-start | bytes 294916
  368.2 2.1 copy-start.31
  368.2 2.1 copy-start.32
  369.7 5.6 collective-permute-start.10
  373.1 2.2 copy-start
  373.1 2.7 copy-start.11
  375.3 2.5 copy-start.24
  375.3 27.6 %collective-permute-start.15 = (bf16[16,16,4736]{2,1,0:T(8,128)(2,1)S(1)}, bf16[16,16,4736]{2,1,0:T(8,128)(2,1)}, u32[]{:S(2)}, u32[]{:S(2)}) collective-permute-start(bf16[16,16,4736]{2,1,0:T(8,128)(2,1)S(1)} %select_bitcast_fusion), channel_id=1, source_target_pairs={{0,1},{1,0},{2,3},{3,2},{4,5},{5,4},{6,7},{7,6},{8,9},{9,8},{10,11... | collective-permute-start | bytes 7274504 | tf_op jit(solution)/shard_map/ppermute | solution.py:594
  376.1 14.3 %copy-start.27 = (f32[512,16]{0,1:T(8,128)S(1)}, f32[512,16]{0,1:T(8,128)}, u32[]{:S(2)}) copy-start(f32[512,16]{0,1:T(8,128)} %param.32) | copy-start | bytes 98308
  376.1 15.1 %copy-start.17 = (f32[16,1536]{1,0:T(8,128)S(1)}, f32[16,1536]{1,0:T(8,128)}, u32[]{:S(2)}) copy-start(f32[16,1536]{1,0:T(8,128)} %get-tuple-element.246) | copy-start | bytes 294916
  376.2 11.8 %collective-permute-start.11 = (bf16[8,16,1664]{2,1,0:T(8,128)(2,1)S(1)}, bf16[8,16,1664]{2,1,0:T(8,128)(2,1)S(1)}, u32[]{:S(2)}, u32[]{:S(2)}) collective-permute-start(bf16[8,16,1664]{2,1,0:T(8,128)(2,1)S(1)} %fusion.22), channel_id=1, source_target_pairs={{0,2},{1,3},{2,0},{3,1},{4,6},{5,7},{6,4},{7,5},{8,10},{9,11},{10,... | collective-permute-start | bytes 1277960 | tf_op jit(solution)/shard_map/ppermute | solution.py:594
  388.9 13.0 %collective-permute-start.12 = (bf16[4,16,1664]{2,1,0:T(8,128)(2,1)}, bf16[4,16,1664]{2,1,0:T(8,128)(2,1)}, u32[]{:S(2)}, u32[]{:S(2)}) collective-permute-start(bf16[4,16,1664]{2,1,0:T(8,128)(2,1)} %fusion.32), channel_id=1, source_target_pairs={{0,4},{1,5},{2,6},{3,7},{4,0},{5,1},{6,2},{7,3},{8,12},{9,13},{10,... | collective-permute-start | bytes 638984 | tf_op jit(solution)/shard_map/ppermute | solution.py:594
  395.7 7.3 %slice-start = ((s8[4849664]{0:T(1024)(128)(4,1)}), s8[4194304]{0:T(1024)(128)(4,1)S(1)}, s32[]{:S(2)}) async-start(s8[4849664]{0:T(1024)(128)(4,1)} %bitcast.334), calls=%async_computation | async-start | bytes 8388608
  395.7 7.3 %slice-start.1 = ((s8[4849664]{0:T(1024)(128)(4,1)}), s8[655360]{0:T(1024)(128)(4,1)S(1)}, s32[]{:S(2)}) async-start(s8[4849664]{0:T(1024)(128)(4,1)} %bitcast.334), calls=%async_computation.1 | async-start | bytes 1310720
  405.6 2.2 copy-start.1
  409.0 27.8 %collective-permute-start.16 = (bf16[8,16,4736]{2,1,0:T(8,128)(2,1)}, bf16[8,16,4736]{2,1,0:T(8,128)(2,1)}, u32[]{:S(2)}, u32[]{:S(2)}) collective-permute-start(bf16[8,16,4736]{2,1,0:T(8,128)(2,1)} %fusion.6), channel_id=1, source_target_pairs={{0,2},{1,3},{2,0},{3,1},{4,6},{5,7},{6,4},{7,5},{8,10},{9,11},{10,... | collective-permute-start | bytes 3637256 | tf_op jit(solution)/shard_map/ppermute | solution.py:594
  411.8 2.9 copy-start.3
  413.4 3.3 copy-start.5
  416.8 9.6 %collective-permute-start.13 = (bf16[2,16,1664]{2,1,0:T(8,128)(2,1)}, bf16[2,16,1664]{2,1,0:T(8,128)(2,1)S(1)}, u32[]{:S(2)}, u32[]{:S(2)}) collective-permute-start(bf16[2,16,1664]{2,1,0:T(8,128)(2,1)} %copy.371), channel_id=1, source_target_pairs={{0,8},{1,9},{2,10},{3,11},{4,12},{5,13},{6,14},{7,15},{8,0},{9,1},... | collective-permute-start | bytes 319496 | tf_op jit(solution)/shard_map/ppermute | solution.py:594
  436.8 3.9 copy-start.6
  440.1 1.5 copy-start.4
  440.2 13.6 %collective-permute-start.17 = (bf16[4,16,4736]{2,1,0:T(8,128)(2,1)S(1)}, bf16[4,16,4736]{2,1,0:T(8,128)(2,1)S(1)}, u32[]{:S(2)}, u32[]{:S(2)}) collective-permute-start(bf16[4,16,4736]{2,1,0:T(8,128)(2,1)S(1)} %fusion.20), channel_id=1, source_target_pairs={{0,4},{1,5},{2,6},{3,7},{4,0},{5,1},{6,2},{7,3},{8,12},{9,13},{10,... | collective-permute-start | bytes 1818632 | tf_op jit(solution)/shard_map/ppermute | solution.py:594
  466.7 11.7 %collective-permute-start.18 = (bf16[2,16,4736]{2,1,0:T(8,128)(2,1)S(1)}, bf16[2,16,4736]{2,1,0:T(8,128)(2,1)S(1)}, u32[]{:S(2)}, u32[]{:S(2)}) collective-permute-start(bf16[2,16,4736]{2,1,0:T(8,128)(2,1)S(1)} %copy.387), channel_id=1, source_target_pairs={{0,8},{1,9},{2,10},{3,11},{4,12},{5,13},{6,14},{7,15},{8,0},{9,1},... | collective-permute-start | bytes 909320 | tf_op jit(solution)/shard_map/ppermute | solution.py:594
  468.5 25.5 %collective-permute-start.14 = (bf16[1,16,1664]{1,2,0:T(8,128)(2,1)}, bf16[1,16,1664]{1,2,0:T(8,128)(2,1)S(1)}, u32[]{:S(2)}, u32[]{:S(2)}) collective-permute-start(bf16[1,16,1664]{1,2,0:T(8,128)(2,1)} %fusion.23), channel_id=1, source_target_pairs={{0,16},{1,17},{2,18},{3,19},{4,20},{5,21},{6,22},{7,23},{8,24},{9,... | collective-permute-start | bytes 159752 | tf_op jit(solution)/shard_map/ppermute | solution.py:594
  485.5 2.2 copy-start.2
  488.4 7.5 %collective-permute-start.19 = (bf16[1,16,4736]{2,1,0:T(8,128)(2,1)S(1)}, bf16[1,16,4736]{2,1,0:T(8,128)(2,1)S(1)}, u32[]{:S(2)}, u32[]{:S(2)}) collective-permute-start(bf16[1,16,4736]{2,1,0:T(8,128)(2,1)S(1)} %copy.389), channel_id=1, source_target_pairs={{0,16},{1,17},{2,18},{3,19},{4,20},{5,21},{6,22},{7,23},{8,24},{9,... | collective-permute-start | bytes 454664 | tf_op jit(solution)/shard_map/ppermute | solution.py:594
  501.2 34.8 %copy-start.8 = (f32[2048,16]{1,0:T(8,128)S(1)}, f32[2048,16]{1,0:T(8,128)}, u32[]{:S(2)}) copy-start(f32[2048,16]{1,0:T(8,128)} %copy-done.7) | copy-start | bytes 393220
  502.2 40.0 %copy-start.18 = (f32[128,16]{1,0:T(8,128)}, f32[128,16]{1,0:T(8,128)S(1)}, u32[]{:S(2)}) copy-start(f32[128,16]{1,0:T(8,128)S(1)} %fusion.35) | copy-start | bytes 24580
  510.1 1.3 collective-permute-start.20
  512.0 3.7 collective-permute-start.21
  516.4 3.7 collective-permute-start.22
  520.7 3.7 collective-permute-start.23
  525.1 4.6 collective-permute-start.24
  542.2 6.7 %copy-start.12 = (f32[2048,16]{1,0:T(8,128)S(1)}, f32[2048,16]{1,0:T(8,128)}, u32[]{:S(2)}) copy-start(f32[2048,16]{1,0:T(8,128)} %get-tuple-element.214) | copy-start | bytes 393220
  549.8 4.5 copy-start.14
  549.8 11.6 %copy-start.10 = (f32[16,1664]{0,1:T(8,128)S(1)}, f32[16,1664]{0,1:T(8,128)}, u32[]{:S(2)}) copy-start(f32[16,1664]{0,1:T(8,128)} %copy-done.9) | copy-start | bytes 319492
  563.7 2.7 copy-start.28
  563.7 2.7 copy-start.29
  563.8 2.7 copy-start.30
  563.8 4.0 copy-start.33
  563.8 4.0 copy-start.34
  563.8 4.0 copy-start.35
  (1 other events, 1.0 us)

commit v2 on v1

--- a/solution.py
+++ b/solution.py
@@ -19,6 +19,9 @@
 NEG = -1e30
 EPS = 1e-05
 SCALE = HDIM ** (-0.5)
+LANES = 128
+BIAS = 64
+BACK = (1, 3, 2, 1, 1)
 
 
 def dot(a, b, ca, cb):
@@ -51,8 +54,6 @@
     extra,
     tok_ref,
     state_ref,
-    memb_ref,
-    vec_ref,
     inw_ref,
     qkv_ref,
     pt_ref,
@@ -62,15 +63,21 @@
     vt_ref,
     sk_ref,
     ot_ref,
+    side_ref,
 ):
     length, width = tok_ref.shape[1:]
     heads = width // HDIM
     rows = length + PAD
-    memory = (state_ref[0].astype(FL) + memb_ref[...]).astype(BF)
+
+    @pl.when(pl.program_id(0) == 0)
+    def _():
+        side_ref[...] = inw_ref[:, 3 * width :].astype(FL).T
+
+    memory = (state_ref[0].astype(FL) + side_ref[:PAD]).astype(BF)
     inputs = jnp.concatenate([tok_ref[0], memory], axis=0)
-    qkv_ref[0, :, :width] = ((dot(inputs, inw_ref[:, :width], 1, 0) + vec_ref[0:1, :]) * SCALE).astype(BF)
+    qkv_ref[0, :, :width] = ((dot(inputs, inw_ref[:, :width], 1, 0) + side_ref[PAD : PAD + 1]) * SCALE).astype(BF)
     qkv_ref[0, :, width : 2 * width] = dot(inputs, inw_ref[:, width : 2 * width], 1, 0).astype(BF)
-    qkv_ref[0, :, 2 * width :] = (dot(inputs, inw_ref[:, 2 * width :], 1, 0) + vec_ref[1:2, :]).astype(BF)
+    qkv_ref[0, :, 2 * width :] = (dot(inputs, inw_ref[:, 2 * width : 3 * width], 1, 0) + side_ref[PAD + 1 : PAD + 2]).astype(BF)
     vt_ref[...] = qkv_ref[0, :length, 2 * width :].T
 
     key_place = lax.broadcasted_iota(jnp.int32, (heads * PAD, 1), 0) % PAD
@@ -134,7 +141,7 @@
     mixed_ref[0, :length, :] = om_t.astype(BF).T
 
 
-def attend(extra, tok, state, memb, vecs, in_w):
+def attend(extra, tok, state, near):
     count, length, width = tok.shape
     heads = width // HDIM
     rows = length + PAD
@@ -148,9 +155,7 @@
         in_specs=[
             one(length, width),
             one(PAD, width),
-            whole(PAD, width),
-            whole(8, width),
-            whole(width, 3 * width),
+            whole(width, 3 * width + LANES),
         ],
         out_specs=[
             one(rows, 3 * width),
@@ -170,10 +175,11 @@
             pltpu.VMEM((width, length), BF),
             pltpu.VMEM((heads * PAD, length), FL),
             pltpu.VMEM((width, length), FL),
+            pltpu.VMEM((LANES, width), FL),
         ],
         compiler_params=pltpu.CompilerParams(vmem_limit_bytes=56 << 20),
         name="attend",
-    )(tok, state, memb, vecs, in_w)
+    )(tok, state, near)
 
 
 def norm_rows(x):
@@ -196,10 +202,10 @@
 
 
 def feed_kernel(
+    devices,
     tok_ref,
     state_ref,
-    memb_ref,
-    vec_ref,
+    small_ref,
     upb_ref,
     wide_ref,
     mixed_ref,
@@ -208,8 +214,8 @@
     one_ref,
     gm_ref,
     gwide_ref,
-    gvec_ref,
-    gupb_ref,
+    side_ref,
+    gside_ref,
     acc_ref,
     sums_ref,
     upb_sum_ref,
@@ -235,6 +241,7 @@
     length, width = tok_ref.shape[1:]
     hid = upb_ref.shape[1]
     rows = length + PAD
+    shard, per = width // devices, hid // devices
     up = slice(0, hid)
     down = slice(hid, 2 * hid)
     outw = slice(2 * hid, 2 * hid + width)
@@ -244,12 +251,13 @@
         acc_ref[...] = jnp.zeros_like(acc_ref)
         sums_ref[...] = jnp.zeros_like(sums_ref)
         upb_sum_ref[...] = jnp.zeros_like(upb_sum_ref)
+        side_ref[...] = small_ref[...].astype(FL).T
 
     att_ref[...] = dot(mixed_ref[0], wide_ref[:, outw], 1, 1)
     att_ref[:length] += tok_ref[0].astype(FL)
-    att_ref[length:] += state_ref[0].astype(FL) + memb_ref[...]
-    bias_att, bias_ffn = vec_ref[2:3, :], vec_ref[3:4, :]
-    gain_one, shift_one, gain_two, shift_two = (vec_ref[i : i + 1, :] for i in range(4, 8))
+    att_ref[length:] += state_ref[0].astype(FL) + side_ref[:PAD]
+    bias_att, bias_ffn = side_ref[PAD + 2 : PAD + 3], side_ref[PAD + 3 : PAD + 4]
+    gain_one, shift_one, gain_two, shift_two = (side_ref[PAD + i : PAD + i + 1] for i in range(4, 8))
 
     def norm_one(i, carry):
         r = pl.ds(pl.multiple_of(i * ROWS, ROWS), ROWS)
@@ -335,12 +343,18 @@
             gwide_ref[:, c] = (acc_ref[:, c] + dot(m_low_ref[...], m_gpre_ref[:, c], 0, 0)).astype(BF)
             gwide_ref[:, d] = (acc_ref[:, d] + dot(m_gb_ref[...], m_hidden_ref[:, c], 0, 0)).astype(BF)
         gwide_ref[:, outw] = (acc_ref[:, outw] + dot(m_ga_ref[...], m_mixed_ref[...], 0, 0)).astype(BF)
+        side_ref[...] = jnp.zeros_like(side_ref)
         for i in range(8):
-            gvec_ref[i : i + 1, :] = jnp.sum(sums_ref[8 * i : 8 * i + 8], axis=0, keepdims=True)
-        gupb_ref[...] = jnp.sum(upb_sum_ref[...], axis=0, keepdims=True)
-
-
-def feed(tok, state, memb, vecs, upb, wide, mixed, cot):
+            side_ref[PAD + i : PAD + i + 1] = jnp.sum(sums_ref[8 * i : 8 * i + 8], axis=0, keepdims=True)
+        gside_ref[...] = side_ref[...].T
+        bias = jnp.sum(upb_sum_ref[...], axis=0, keepdims=True)
+        for i in range(devices):
+            piece = bias[:, i * per : (i + 1) * per]
+            gside_ref[i * shard : i * shard + 1, BIAS : BIAS + per] = piece
+        gwide_ref[:, 2 * hid + width :] = gside_ref[...].astype(BF)
+
+
+def feed(devices, tok, state, small, upb, wide, mixed, cot):
     count, length, width = tok.shape
     rows = length + PAD
     hid = upb.shape[1]
@@ -350,13 +364,12 @@
     final = lambda *dims: pl.BlockSpec(dims, lambda b: (0,) * len(dims))
     vm = pltpu.VMEM
     return pl.pallas_call(
-        feed_kernel,
+        partial(feed_kernel, devices),
         grid=(count,),
         in_specs=[
             one(length, width),
             one(PAD, width),
-            whole(PAD, width),
-            whole(8, width),
+            whole(width, LANES),
             whole(1, hid),
             whole(width, cols),
             one(rows, width),
@@ -366,19 +379,17 @@
             one(rows, width),
             one(rows, width),
             one(rows, width),
-            final(width, cols),
-            final(8, width),
-            final(1, hid),
+            final(width, cols + LANES),
         ],
         out_shape=[
             jax.ShapeDtypeStruct((count, rows, width), BF),
             jax.ShapeDtypeStruct((count, rows, width), FL),
             jax.ShapeDtypeStruct((count, rows, width), BF),
-            jax.ShapeDtypeStruct((width, cols), BF),
-            jax.ShapeDtypeStruct((8, width), FL),
-            jax.ShapeDtypeStruct((1, hid), FL),
+            jax.ShapeDtypeStruct((width, cols + LANES), BF),
         ],
         scratch_shapes=[
+            vm((LANES, width), FL),
+            vm((width, LANES), FL),
             vm((width, cols), FL),
             vm((64, width), FL),
             vm((8, hid), FL),
@@ -401,45 +412,26 @@
         ],
         compiler_params=pltpu.CompilerParams(vmem_limit_bytes=60 << 20),
         name="feed",
-    )(tok, state, memb, vecs, upb, wide, mixed, cot)
+    )(tok, state, small, upb, wide, mixed, cot)
 
 
 def return_kernel(
-    tok_ref,
-    state_ref,
-    memb_ref,
-    inw_ref,
     qkv_ref,
     pt_ref,
     ptk_ref,
     ptq_ref,
     gm_ref,
-    one_ref,
-    grad_ref,
-    gin_ref,
-    acc_ref,
-    sums_ref,
+    dj_ref,
     kt_ref,
     dpk_ref,
     dsk_ref,
     dqt_ref,
     dk_ref,
     dv_ref,
-    dj_ref,
-    m_in_ref,
-    m_dj_ref,
-    side_ref,
 ):
-    step = pl.program_id(0)
-    last = pl.num_programs(0) - 1
-    length, width = tok_ref.shape[1:]
+    width = gm_ref.shape[2]
+    length = gm_ref.shape[1] - PAD
     heads = width // HDIM
-
-    @pl.when(step == 0)
-    def _():
-        acc_ref[...] = jnp.zeros_like(acc_ref)
-        sums_ref[...] = jnp.zeros_like(sums_ref)
-        side_ref[...] = jnp.zeros_like(side_ref)
 
     kt_ref[...] = qkv_ref[0, :length, width : 2 * width].T
     q_mem = spread(qkv_ref[0, length:, :width], heads)
@@ -454,13 +446,13 @@
     dsq = (tq - pq * jnp.sum(tq, axis=0, keepdims=True)).astype(BF)
     dv_ref[...] = dot(ptq_ref[0], do_mem, 1, 0)
     dk_ref[...] = dot(dsq, q_mem, 1, 0)
-    dj_ref[length:, :width] = (fold(dot(dsq, qkv_ref[0, :, width : 2 * width], 0, 0), heads) * SCALE).astype(BF)
+    dq_mem = fold(dot(dsq, qkv_ref[0, :, width : 2 * width], 0, 0), heads)
+    dj_ref[0, length:, :width] = (dq_mem * SCALE).astype(BF)
 
     masks = pair_masks(2 * HDIM)
 
     def pair(p, carry):
         lanes = pl.ds(pl.multiple_of(p * 2 * HDIM, 2 * HDIM), 2 * HDIM)
-        key_lanes = pl.ds(pl.multiple_of(width + p * 2 * HDIM, 2 * HDIM), 2 * HDIM)
         val_lanes = pl.ds(pl.multiple_of(2 * width + p * 2 * HDIM, 2 * HDIM), 2 * HDIM)
         vp = qkv_ref[0, :length, val_lanes]
         dop = gm_ref[0, :length, lanes]
@@ -494,124 +486,289 @@
     lax.fori_loop(0, heads // 2, pair, 0)
 
     dq_t = dqt_ref[...] + dot(k_mem, dsk_ref[...], 0, 0)
-    dj_ref[:length, :width] = (dq_t * SCALE).astype(BF).T
+    dj_ref[0, :length, :width] = (dq_t * SCALE).astype(BF).T
     dv_ref[length:, :] += fold(dot(ptk_ref[0], gm_ref[0, :length, :], 1, 0), heads)
     dk_ref[length:, :] += fold(dot(dsk_ref[...], qkv_ref[0, :length, :width], 1, 0), heads)
-    dj_ref[:, width : 2 * width] = dk_ref[...].astype(BF)
-    dj_ref[:, 2 * width :] = dv_ref[...].astype(BF)
-    sums_ref[0:8] += by_eight(dj_ref[:, :width].astype(FL))
-    sums_ref[8:16] += by_eight(dj_ref[:, 2 * width :].astype(FL))
-
-    mem = pl.ds(pl.multiple_of(step * PAD, PAD), PAD)
-    m_in_ref[mem, :] = (state_ref[0].astype(FL) + memb_ref[...]).astype(BF)
-    m_dj_ref[mem, :] = dj_ref[length:, :]
-    for j in range(3):
-        c = slice(j * width, (j + 1) * width)
-        acc_ref[:, c] += dot(tok_ref[0], dj_ref[:length, c], 0, 0)
-    grad_ref[0] = one_ref[0, :length, :] + dot(dj_ref[:length, :], inw_ref[...], 1, 1)
-    side_ref[0:PAD, :] += one_ref[0, length:, :] + dot(dj_ref[length:, :], inw_ref[...], 1, 1)
-
-    @pl.when(step == last)
-    def _():
-        for j in range(3):
-            c = slice(j * width, (j + 1) * width)
-            gin_ref[:, c] = (acc_ref[:, c] + dot(m_in_ref[...], m_dj_ref[:, c], 0, 0)).astype(BF)
-        side_ref[PAD : PAD + 1, :] = jnp.sum(sums_ref[0:8], axis=0, keepdims=True)
-        side_ref[PAD + 1 : PAD + 2, :] = jnp.sum(sums_ref[8:16], axis=0, keepdims=True)
-        gin_ref[:, 3 * width :] = side_ref[...].T.astype(BF)
-
-
-def go_back(tok, state, memb, in_w, qkv, pt, ptk, ptq, gm, one_grad):
-    count, length, width = tok.shape
-    rows = length + PAD
+    dj_ref[0, :, width : 2 * width] = dk_ref[...].astype(BF)
+    dj_ref[0, :, 2 * width :] = dv_ref[...].astype(BF)
+
+
+def go_back(begin, count, qkv, pt, ptk, ptq, gm):
+    rows, width = gm.shape[1:]
+    length = rows - PAD
     heads = width // HDIM
-    one = lambda *dims: pl.BlockSpec((1,) + dims, lambda b: (b,) + (0,) * len(dims))
-    whole = lambda *dims: pl.BlockSpec(dims, lambda b: (0,) * len(dims), pipeline_mode=pl.Buffered(1))
-    final = lambda *dims: pl.BlockSpec(dims, lambda b: (0,) * len(dims))
+    one = lambda *dims: pl.BlockSpec((1,) + dims, lambda b: (b + begin,) + (0,) * len(dims))
     vm = pltpu.VMEM
     return pl.pallas_call(
         return_kernel,
         grid=(count,),
         in_specs=[
-            one(length, width),
-            one(PAD, width),
-            whole(PAD, width),
-            whole(width, 3 * width),
             one(rows, 3 * width),
             one(*pt.shape[1:]),
             one(heads * PAD, length),
             one(rows, heads * PAD),
             one(rows, width),
-            one(rows, width),
-        ],
-        out_specs=[one(length, width), final(width, 3 * width + 128)],
-        out_shape=[
-            jax.ShapeDtypeStruct((count, length, width), FL),
-            jax.ShapeDtypeStruct((width, 3 * width + 128), BF),
-        ],
+        ],
+        out_specs=pl.BlockSpec((1, rows, 3 * width), lambda b: (b, 0, 0)),
+        out_shape=jax.ShapeDtypeStruct((count, rows, 3 * width), BF),
         scratch_shapes=[
-            vm((width, 3 * width), FL),
-            vm((16, width), FL),
             vm((width, length), BF),
             vm((heads * PAD, length), FL),
             vm((heads * PAD, length), BF),
             vm((width, length), FL),
             vm((rows, width), FL),
             vm((rows, width), FL),
-            vm((rows, 3 * width), BF),
+        ],
+        compiler_params=pltpu.CompilerParams(vmem_limit_bytes=48 << 20),
+        cost_estimate=pl.CostEstimate(flops=count * 10**10, bytes_accessed=count * 10**7, transcendentals=0),
+        name="go_back",
+    )(qkv, pt, ptk, ptq, gm)
+
+
+def weigh_kernel(
+    begins,
+    tok_ref,
+    state_ref,
+    one_ref,
+    inw_ref,
+    *refs,
+):
+    dj_refs, refs = refs[: len(begins)], refs[len(begins) :]
+    gin_ref, acc_ref, sums_ref, m_in_ref, m_dj_ref, side_ref, memb_ref = refs
+    step = pl.program_id(0)
+    last = pl.num_programs(0) - 1
+    length, width = tok_ref.shape[1:]
+    ends = begins[1:] + [last + 1]
+
+    @pl.when(step == 0)
+    def _():
+        acc_ref[...] = jnp.zeros_like(acc_ref)
+        sums_ref[...] = jnp.zeros_like(sums_ref)
+        side_ref[...] = jnp.zeros_like(side_ref)
+        memb_ref[...] = inw_ref[:, 3 * width :].astype(FL).T
+
+    mem = pl.ds(pl.multiple_of(step * PAD, PAD), PAD)
+    m_in_ref[mem, :] = (state_ref[0].astype(FL) + memb_ref[:PAD]).astype(BF)
+    side_ref[0:PAD, :] += one_ref[0]
+    for g, dj_ref in enumerate(dj_refs):
+
+        @pl.when((step >= begins[g]) & (step < ends[g]))
+        def _(dj_ref=dj_ref):
+            m_dj_ref[mem, :] = dj_ref[0, length:, :]
+            sums_ref[0:8] += by_eight(dj_ref[0, :, :width].astype(FL))
+            sums_ref[8:16] += by_eight(dj_ref[0, :, 2 * width :].astype(FL))
+            for j in range(3):
+                c = slice(j * width, (j + 1) * width)
+                acc_ref[:, c] += dot(tok_ref[0], dj_ref[0, :length, c], 0, 0)
+
+    @pl.when(step == last)
+    def _():
+        for j in range(3):
+            c = slice(j * width, (j + 1) * width)
+            gin_ref[:, c] = (acc_ref[:, c] + dot(m_in_ref[...], m_dj_ref[:, c], 0, 0)).astype(BF)
+        back = dot(m_dj_ref[...], inw_ref[:, : 3 * width], 1, 1)
+        side_ref[0:PAD, :] += jnp.sum(back.reshape(last + 1, PAD, width), axis=0)
+        side_ref[PAD : PAD + 1, :] = jnp.sum(sums_ref[0:8], axis=0, keepdims=True)
+        side_ref[PAD + 1 : PAD + 2, :] = jnp.sum(sums_ref[8:16], axis=0, keepdims=True)
+        gin_ref[:, 3 * width :] = side_ref[...].T.astype(BF)
+
+
+def weigh(tok, state, near, one_grad, djs, begins):
+    count, length, width = tok.shape
+    rows = length + PAD
+    one = lambda *dims: pl.BlockSpec((1,) + dims, lambda b: (b,) + (0,) * len(dims))
+    whole = lambda *dims: pl.BlockSpec(dims, lambda b: (0,) * len(dims), pipeline_mode=pl.Buffered(1))
+    final = lambda *dims: pl.BlockSpec(dims, lambda b: (0,) * len(dims))
+    part = lambda g: pl.BlockSpec(
+        (1, rows, 3 * width), lambda b: (jnp.clip(b - begins[g], 0, djs[g].shape[0] - 1), 0, 0)
+    )
+    vm = pltpu.VMEM
+    return pl.pallas_call(
+        partial(weigh_kernel, begins),
+        grid=(count,),
+        in_specs=[
+            one(length, width),
+            one(PAD, width),
+            pl.BlockSpec((1, PAD, width), lambda b: (b, length // PAD, 0)),
+            whole(width, 3 * width + LANES),
+        ]
+        + [part(g) for g in range(len(djs))],
+        out_specs=final(width, 3 * width + LANES),
+        out_shape=jax.ShapeDtypeStruct((width, 3 * width + LANES), BF),
+        scratch_shapes=[
+            vm((width, 3 * width), FL),
+            vm((16, width), FL),
             vm((count * PAD, width), BF),
             vm((count * PAD, 3 * width), BF),
-            vm((128, width), FL),
-        ],
-        compiler_params=pltpu.CompilerParams(vmem_limit_bytes=60 << 20),
-        name="go_back",
-    )(tok, state, memb, in_w, qkv, pt, ptk, ptq, gm, one_grad)
-
-
-def gather(x, devices, index):
+            vm((LANES, width), FL),
+            vm((LANES, width), FL),
+        ],
+        compiler_params=pltpu.CompilerParams(vmem_limit_bytes=48 << 20),
+        cost_estimate=pl.CostEstimate(flops=count * 10**9, bytes_accessed=count * 3 * 10**6, transcendentals=0),
+        name="weigh",
+    )(tok, state, one_grad, near, *djs)
+
+
+def descend_kernel(one_ref, dj_ref, inw_ref, grad_ref):
+    width = one_ref.shape[2]
+    grad_ref[0] = one_ref[0] + dot(dj_ref[0], inw_ref[:, : 3 * width], 1, 1)
+
+
+def descend(total, begin, one_grad, dj, near, into):
+    count, rows, wide = dj.shape
+    width = one_grad.shape[2]
+    length = rows - PAD
+    shift = lambda *dims: pl.BlockSpec((1,) + dims, lambda b: (b + begin, 0, 0))
+    kept = () if into is None else (into,)
+
+    def kernel(one_ref, dj_ref, inw_ref, *rest):
+        descend_kernel(one_ref, dj_ref, inw_ref, rest[-1])
+
+    return pl.pallas_call(
+        kernel,
+        grid=(count,),
+        in_specs=[
+            shift(length, width),
+            pl.BlockSpec((1, length, wide), lambda b: (b, 0, 0)),
+            pl.BlockSpec((width, wide + LANES), lambda b: (0, 0), pipeline_mode=pl.Buffered(1)),
+        ]
+        + [pl.BlockSpec(memory_space=pl.ANY)] * len(kept),
+        out_specs=shift(length, width),
+        out_shape=jax.ShapeDtypeStruct((total, length, width), FL),
+        input_output_aliases={3: 0} if kept else {},
+        compiler_params=pltpu.CompilerParams(vmem_limit_bytes=32 << 20),
+        cost_estimate=pl.CostEstimate(flops=count * 10**9, bytes_accessed=count * 4 * 10**6, transcendentals=0),
+        name="descend",
+    )(one_grad, dj, near, *kept)
+
+
+def pack_kernel(in_ref, up_ref, down_ref, out_ref, vec_ref, bias_ref, mem_ref, near_ref, far_ref, flip_ref):
+    shard, cols = in_ref.shape
+    hid, width = up_ref.shape[1], out_ref.shape[1]
+    flip_ref[...] = jnp.zeros_like(flip_ref)
+    flip_ref[PAD : PAD + 8, :shard] = vec_ref[...]
+    flip_ref[...] = flip_ref[...].T
+    flip_ref[:shard, : mem_ref.shape[1]] = mem_ref[...]
+    flip_ref[0:1, BIAS : BIAS + bias_ref.shape[1]] = bias_ref[...]
+    near_ref[:, :cols] = in_ref[...].astype(BF)
+    near_ref[:, cols:] = flip_ref[:shard].astype(BF)
+    far_ref[:, :hid] = up_ref[...].astype(BF)
+    far_ref[:, hid : 2 * hid] = down_ref[...].astype(BF)
+    far_ref[:, 2 * hid :] = out_ref[...].astype(BF)
+
+
+def pack(in_w, up_w, down_t, out_t, vectors, bias, mem_t):
+    shard, cols = in_w.shape
+    wide = 2 * up_w.shape[1] + out_t.shape[1]
+    return pl.pallas_call(
+        pack_kernel,
+        out_shape=[
+            jax.ShapeDtypeStruct((shard, cols + LANES), BF),
+            jax.ShapeDtypeStruct((shard, wide), BF),
+        ],
+        scratch_shapes=[pltpu.VMEM((LANES, LANES), FL)],
+        name="pack",
+    )(in_w, up_w, down_t, out_t, vectors, bias, mem_t)
+
+
+def square_kernel(cols, near_ref, far_ref, sum_ref):
+    wide = far_ref.shape[1] - LANES
+    near, far = near_ref[:, :cols], far_ref[:, :wide]
+    side = near_ref[:, cols:] + far_ref[:, wide:]
+    total = jnp.sum(near * near) + jnp.sum(far * far) + jnp.sum(side * side)
+    sum_ref[...] = jnp.full(sum_ref.shape, total, FL)
+
+
+def adam_kernel(sizes, rates, decays, near_ref, far_ref, total_ref, *refs):
+    cols, hid, width = sizes
+    state_refs, new_refs, norm_ref, flip_ref = refs[:21], refs[21:42], refs[42], refs[43]
+    shard = near_ref.shape[0]
+    norm = jnp.sqrt(total_ref[...])
+    norm_ref[...] = norm
+    factor = (1.0 / jnp.maximum(norm, 1.0))[0:1, 0:1]
+    side = near_ref[:, cols:] + far_ref[:, 2 * hid + width :]
+    flip_ref[...] = jnp.zeros_like(flip_ref)
+    flip_ref[:shard] = side
+    turned = flip_ref[...].T
+    bias = pltpu.roll(side, LANES - BIAS, 1)
+    grads = (
+        near_ref[:, :cols],
+        far_ref[:, 2 * hid : 2 * hid + width],
+        far_ref[:, :hid],
+        far_ref[:, hid : 2 * hid],
+        turned[PAD : PAD + 8, :shard],
+        bias[0:1, : state_refs[15].shape[1]],
+        side[:, : state_refs[18].shape[1]],
+    )
+    correction = 1.0 - 0.5**STEP
+    for i in range(7):
+        weight, first, second = (state_refs[3 * i + k][...] for k in range(3))
+        grad = grads[i] * factor
+        first_new = 0.5 * first + 0.5 * grad
+        second_new = 0.5 * second + 0.5 * grad * grad
+        step = first_new / correction / (jnp.sqrt(second_new / correction) + 1e-08)
+        new_refs[3 * i][...] = weight - rates[i] * (step + decays[i] * weight)
+        new_refs[3 * i + 1][...] = first_new
+        new_refs[3 * i + 2][...] = second_new
+
+
+def exchange(x, bit, devices):
+    return lax.ppermute(x, AXES, [(i, i ^ bit) for i in range(devices)])
+
+
+def beside(got, sent, work):
+    if work is None:
+        return got, None
+    made = work(lambda value: lax.optimization_barrier((value, sent))[0])
+    return lax.optimization_barrier((got, made))
+
+
+def gather(x, devices, index, works):
     rows, cols = x.shape
     held = x[None]
     bit = devices // 2
+    results = []
     while bit:
-        got = lax.ppermute(held, AXES, [(i, i ^ bit) for i in range(devices)])
+        got = exchange(held, bit, devices)
+        got, made = beside(got, held, works.get(bit))
+        results.append(made)
         upper = (index & bit) != 0
         held = jnp.stack([jnp.where(upper, got, held), jnp.where(upper, held, got)], axis=1)
         held = held.reshape(-1, rows, cols)
         bit //= 2
-    return held.reshape(devices * rows, cols)
-
-
-def scatter_sum(x, devices, index):
+    return held.reshape(devices * rows, cols), [made for made in results if made is not None]
+
+
+def halve(held, got, upper):
+    total = held if got is None else held.astype(FL) + got.astype(FL)
+    keep = jnp.where(upper, total[:, 1], total[:, 0])
+    send = jnp.where(upper, total[:, 0], total[:, 1]).astype(BF)
+    return keep, send
+
+
+def scatter_sum(x, devices, index, works):
     total, cols = x.shape
     rows = total // devices
-    held = x
+    held, got = x.reshape(-1, 2, rows, cols), None
     bit = 1
-    while bit < devices:
-        held = held.reshape(-1, 2, rows, cols)
-        upper = (index & bit) != 0
-        keep = jnp.where(upper, held[:, 1], held[:, 0]).astype(FL)
-        send = jnp.where(upper, held[:, 0], held[:, 1]).astype(BF)
-        held = keep + lax.ppermute(send, AXES, [(i, i ^ bit) for i in range(devices)]).astype(FL)
+    results = []
+    for step in range(devices.bit_length() - 1):
+        keep, send = halve(held, got, (index & bit) != 0)
+        got = exchange(send, bit, devices)
+        got, made = beside(got, send, works[step] if step < len(works) else None)
+        results.append(made)
         bit *= 2
-    return held.reshape(rows, cols)
+        if bit < devices:
+            held, got = keep.reshape(-1, 2, rows, cols), got.reshape(-1, 2, rows, cols)
+    return (keep.astype(FL) + got.astype(FL)).reshape(rows, cols), results
 
 
 def butterfly(x, devices):
     bit = 1
     while bit < devices:
-        x = x + lax.ppermute(x, AXES, [(i, i ^ bit) for i in range(devices)])
+        x = x + exchange(x, bit, devices)
         bit *= 2
     return x
-
-
-def adam_step(weight, first, second, grad, rate, decay):
-    first_new = 0.5 * first + 0.5 * grad
-    second_new = 0.5 * second + 0.5 * grad * grad
-    correction = 1.0 - 0.5**STEP
-    weight_new = weight - rate * (
-        first_new / correction / (jnp.sqrt(second_new / correction) + 1e-08) + decay * weight
-    )
-    return (weight_new, first_new, second_new)
 
 
 def per_device(
@@ -649,61 +806,75 @@
     hid = up_weight.shape[1]
     per_bias = up_bias.shape[0] // shard
 
-    small = jnp.concatenate(
-        [
-            memory_embed.T,
-            jnp.zeros((shard, PAD - extra), FL),
-            vectors.T,
-            up_bias.reshape(per_bias, shard).T,
-            jnp.zeros((shard, 128 - PAD - 8 - per_bias), FL),
-        ],
-        axis=1,
+    near, far = pack(
+        in_weight,
+        up_weight,
+        down_weight.T,
+        out_weight.T,
+        vectors,
+        up_bias.reshape(1, -1),
+        memory_embed.T,
     )
-    near = jnp.concatenate([in_weight, small], axis=1).astype(BF)
-    far = jnp.concatenate([up_weight, down_weight.T, out_weight.T], axis=1).astype(BF)
-    near = gather(near, devices, index)
-    wide = gather(far, devices, index)
-    side = near[:, 3 * width :].astype(FL).T
-    memb = side[:PAD]
-    vecs = side[PAD : PAD + 8]
-    upb = side[PAD + 8 : PAD + 8 + per_bias].reshape(per_bias, devices, shard)
-    upb = upb.transpose(1, 0, 2).reshape(1, hid)
-    in_w = near[:, : 3 * width]
+    wide = lax.all_gather(far, AXES, axis=0, tiled=True)
+
+    def align(tie):
+        cot = tie(cotangent).reshape(count, extra + length, width)
+        return jnp.concatenate(
+            [cot[:, extra:], cot[:, :extra], jnp.zeros((count, PAD - extra, width), BF)], axis=1
+        )
+
+    near, (cot,) = gather(near, devices, index, {2: align})
+    small = near[:, 3 * width :]
+    upb = small.reshape(devices, shard, LANES)[:, 0, BIAS : BIAS + up_bias.shape[0]].astype(FL)
+    upb = upb.reshape(1, hid)
 
     tok = tokens.reshape(count, length, width)
     state = jnp.pad(memory_state.reshape(count, extra, width), ((0, 0), (0, PAD - extra), (0, 0)))
-    cot = cotangent.reshape(count, extra + length, width)
-    cot = jnp.concatenate(
-        [cot[:, extra:], cot[:, :extra], jnp.zeros((count, PAD - extra, width), BF)], axis=1
-    )
-
-    qkv, pt, ptk, ptq, mixed = attend(extra, tok, state, memb, vecs, in_w)
-    out, one_grad, gm, gwide, gvec, gupb = feed(tok, state, memb, vecs, upb, wide, mixed, cot)
-    gupb = gupb.reshape(devices, per_bias, shard).transpose(1, 0, 2).reshape(per_bias, width)
-    gside = jnp.concatenate(
-        [jnp.zeros((PAD, width), FL), gvec, gupb, jnp.zeros((128 - PAD - 8 - per_bias, width), FL)]
-    ).T.astype(BF)
-    gfar = scatter_sum(jnp.concatenate([gwide, gside], axis=1), devices, index)
-    input_grad, gnear = go_back(tok, state, memb, in_w, qkv, pt, ptk, ptq, gm, one_grad)
-    gnear = scatter_sum(gnear, devices, index)
-
-    output = jnp.concatenate([out[:, length : length + extra], out[:, :length]], axis=1)
-    output = output.reshape(micro, local, extra + length, width)
+
+    qkv, pt, ptk, ptq, mixed = attend(extra, tok, state, near)
+    out, one_grad, gm, gwide = feed(devices, tok, state, small, upb, wide, mixed, cot)
+
+    def split(sizes):
+        begins = [0]
+        for size in sizes:
+            begins.append(begins[-1] + size)
+        return list(zip(begins, sizes))
+
+    def back(begin, size):
+        return lambda tie: go_back(begin, size, tie(qkv), pt, ptk, ptq, gm)
+
+    runs = split(BACK) if sum(BACK) == count else split([count])
+    gfar, djs = scatter_sum(gwide, devices, index, [back(*run) for run in runs])
+    djs = djs[: len(runs)]
+    gin = weigh(tok, state, near, one_grad, djs, [begin for begin, _ in runs])
+    grads = []
+
+    def down(picked):
+        def work(tie):
+            for i in picked:
+                into = grads[-1] if grads else None
+                grads.append(descend(count, runs[i][0], one_grad, tie(djs[i]), near, into))
+            return grads[-1]
+
+        return work
+
+    def order(tie):
+        rows = tie(out)
+        rows = jnp.concatenate([rows[:, length : length + extra], rows[:, :length]], axis=1)
+        return rows.reshape(micro, local, extra + length, width).transpose(0, 2, 1, 3)
+
+    cut = len(runs) // 2
+    works = [down(range(cut)), down(range(cut, len(runs))), order]
+    gnear, (_, input_grad, output, *_) = scatter_sum(gin, devices, index, works)
+    output = output.transpose(0, 2, 1, 3)
     input_grad = input_grad.reshape(micro, local, length, width)
 
-    gsmall = (gnear[:, 3 * width :] + gfar[:, 2 * hid + width :]).T
-    grads = (
-        gnear[:, : 3 * width],
-        gfar[:, 2 * hid : 2 * hid + width],
-        gfar[:, :hid],
-        gfar[:, hid : 2 * hid],
-        gsmall[PAD : PAD + 8],
-        gsmall[PAD + 8 : PAD + 8 + per_bias].reshape(up_bias.shape),
-        gsmall[:extra],
-    )
-    squares = sum(jnp.sum(grad * grad) for grad in grads)
-    grad_norm = jnp.sqrt(butterfly(squares.reshape(1, 1), devices)[0, 0])
-    factor = 1.0 / jnp.maximum(grad_norm, 1.0)
+    squares = pl.pallas_call(
+        partial(square_kernel, 3 * width),
+        out_shape=jax.ShapeDtypeStruct((8, LANES), FL),
+        name="squares",
+    )(gnear, gfar)
+    squares = butterfly(squares, devices)
     total_rows = extra + length
     rates = (
         0.5 * width ** (-0.5),
@@ -715,20 +886,30 @@
         0.5,
     )
     decays = (0.1, 0.1, 0.1, 0.1, 0.0, 0.0, 0.0)
+    same = lambda value: value
+    turn = lambda value: value.T
+    flat = lambda value: value.reshape(1, -1)
+    views = (same, turn, same, turn, same, flat, turn)
     states = (
         (in_weight, in_first, in_second),
-        (out_weight.T, out_first.T, out_second.T),
+        (out_weight, out_first, out_second),
         (up_weight, up_first, up_second),
-        (down_weight.T, down_first.T, down_second.T),
+        (down_weight, down_first, down_second),
         (vectors, vectors_first, vectors_second),
         (up_bias, up_bias_first, up_bias_second),
         (memory_embed, memory_first, memory_second),
     )
-    results = []
-    for i, (weight, first, second) in enumerate(states):
-        new = adam_step(weight, first, second, grads[i] * factor, rates[i], decays[i])
-        results.extend(value.T if i in (1, 3) else value for value in new)
-    return (output, input_grad, *results, grad_norm)
+    held = [view(value) for view, group in zip(views, states) for value in group]
+    *new, norm = pl.pallas_call(
+        partial(adam_kernel, (3 * width, hid, width), rates, decays),
+        out_shape=[jax.ShapeDtypeStruct(value.shape, FL) for value in held]
+        + [jax.ShapeDtypeStruct((8, LANES), FL)],
+        scratch_shapes=[pltpu.VMEM((LANES, LANES), FL)],
+        name="adam",
+    )(gnear, gfar, squares, *held)
+    back_views = (same, turn, same, turn, same, lambda value: value.reshape(-1), turn)
+    results = [back_views[i // 3](value) for i, value in enumerate(new)]
+    return (output, input_grad, *results, norm[0, 0])
 
 
 def solution(mesh):

time: 576 us -> 397 us (0.69)
  local copies, waits for them, and re-layouts: 103 us -> 18.3 us
  waiting for transfers between devices: 98.4 us -> 38.5 us
  other arithmetic: 72.2 us -> 23.9 us
  Pallas kernels: 248 us -> 274 us
  starting transfers between devices: 37.7 us -> 20.2 us
    ppermute x25 -> x20, waiting for transfers between devices: 98.4 us -> 38.4 us  [exchange(): return lax.ppermute(x, AXES, [(i, i ^ bit) for i in range(devices)])]
    unnamed x109 -> x41, local copies, waits for them, and re-layouts: 56.3 us -> 5.28 us
    pallas_call x2 -> x15, Pallas kernels: 178 us -> 205 us  [the longest x1 90.3 us: feed(): pl.pallas_call(partial(feed_kernel, devices), grid=(count,), in_specs=[on...]
    ppermute x25 -> x20, starting transfers between devices: 37.7 us -> 20.1 us  [exchange(): return lax.ppermute(x, AXES, [(i, i ^ bit) for i in range(devices)])]
    mul x11 -> x0, local copies, waits for them, and re-layouts: 17.3 us -> none  [the longest x4 7.35 us: adam_step(): first_new = 0.5 * first + 0.5 * grad]
    slice x11 -> x6, local copies, waits for them, and re-layouts: 13.1 us -> 2.62 us  [the longest x1 1.19 us: per_device(): return (output, input_grad, *results, norm[0, 0])]
    transpose x4 -> x0, other arithmetic: 9.22 us -> none  [the longest x2 8.27 us: per_device(): results.extend((value.T if i in (1, 3) else value for value in new))]
    convert_element_type x6 -> x1, local copies, waits for them, and re-layouts: 9.37 us -> 0.9 us  [per_device(): small.reshape(devices, shard, LANES)[:, 0, BIAS:BIAS + up_bias.shape[0]]]
  transfers between devices with their start and end apart: 25 -> 21, of which waited for: 16 -> 13; matrix products, arithmetic and copies ran while one was open for 15% -> 5% of each run, Pallas kernels for 12% -> 42%
where the time goes in v2:
time: 397 us; the launch traced here: 390 us
  Pallas kernels  274 us (69%)
  waiting for transfers between devices  38.5 us (10%)
  other arithmetic  23.9 us (6%)
  starting transfers between devices  20.2 us (5%)
  local copies, waits for them, and re-layouts  18.3 us (5%)
  between operations  15 us (4%)
    pallas_call x1, Pallas kernels, feed(): pl.pallas_call(partial(feed_kernel, devices), grid=(count,), in_specs=[on...  90.3 us
    pallas_call x5, Pallas kernels, go_back(): pl.pallas_call(return_kernel, grid=(count,), in_specs=[one(rows, 3 * widt...  80 us
    pallas_call x1, Pallas kernels, attend(): pl.pallas_call(partial(attend_kernel, extra), grid=(count,), in_specs=[on...  69.4 us
    ppermute x20, waiting for transfers between devices, exchange(): return lax.ppermute(x, AXES, [(i, i ^ bit) for i in range(devices)])  38.4 us
    ppermute x20, starting transfers between devices, exchange(): return lax.ppermute(x, AXES, [(i, i ^ bit) for i in range(devices)])  20.1 us
    pallas_call x1, Pallas kernels, weigh(): pl.pallas_call(partial(weigh_kernel, begins), grid=(count,), in_specs=[on...  15.4 us
    pallas_call x5, Pallas kernels, descend(): pl.pallas_call(kernel, grid=(count,), in_specs=[shift(length, width), pl....  13.2 us
  transfers between devices with their start and end apart: 21, of which 13 were waited for; matrix products, arithmetic and copies ran while one was open for 5% of the time, Pallas kernels for 42%

profile of v2, /device:TPU:0, one launch (start us, length us, event | category | flops | bytes accessed | tf_op | source)
XLA Modules:
  0.0 390.3 jit_solution(3346725399417182094)
XLA Ops:
  7.2 1.8 pack.1
  9.0 4.1 %collective-permute-start = (bf16[1,16,1664]{2,1,0:T(8,128)(2,1)}, bf16[1,16,1664]{2,1,0:T(8,128)(2,1)S(1)}, u32[]{:S(2)}, u32[]{:S(2)}) collective-permute-start(bf16[1,16,1664]{2,1,0:T(8,128)(2,1)} %bitcast.220), channel_id=1, source_target_pairs={{0,16},{1,17},{2,18},{3,19},{4,20},{5,21},{6,22},{7,23},{8,24},{9,... | collective-permute-start | bytes 159752 | tf_op jit(solution)/shard_map/ppermute | solution.py:716
  13.2 2.9 collective-permute-done
  16.0 0.8 select_bitcast_fusion.11
  16.9 1.4 collective-permute-start.1
  18.3 3.4 collective-permute-done.1
  21.8 1.8 collective-permute-start.2
  23.5 5.2 %collective-permute-done.2 = bf16[4,16,1664]{2,1,0:T(8,128)(2,1)S(1)} collective-permute-done((bf16[4,16,1664]{2,1,0:T(8,128)(2,1)S(1)}, bf16[4,16,1664]{2,1,0:T(8,128)(2,1)S(1)}, u32[]{:S(2)}, u32[]{:S(2)}) %collective-permute-start.2) | collective-permute-done | bytes 213024 | tf_op jit(solution)/shard_map/ppermute | solution.py:716
  28.9 1.7 collective-permute-start.3
  30.6 3.0 copy.81
  33.7 1.1 slice.128
  34.8 3.9 %maximum_maximum_fusion.cot_ref = bf16[8,544,512]{2,1,0:T(8,128)(2,1)} fusion(bf16[8,20,512]{2,1,0:T(8,128)(2,1)S(1)} %slice.129, bf16[8,512,512]{2,1,0:T(8,128)(2,1)S(1)} %slice.128, bf16[544]{0:T(1024)(128)(2,1)S(1)} %pad.13.clone), kind=kLoop, calls=%fused_computation.1 | loop fusion | flops 13369344 | bytes 8815680 | tf_op jit(solution)/shard_map/concatenate | solution.py:822
  39.1 0.5 copy-done.11
  39.7 0.7 pad.4.state_ref
  40.4 1.1 collective-permute-done.4
  42.2 0.9 reshape.326.upb_ref
  43.2 69.4 %attend.1 = (bf16[8,544,1536]{2,1,0:T(8,128)(2,1)}, bf16[8,8,768,256]{3,2,1,0:T(8,128)(2,1)}, bf16[8,256,512]{2,1,0:T(8,128)(2,1)}, bf16[8,544,256]{2,1,0:T(8,128)(2,1)}, bf16[8,544,512]{2,1,0:T(8,128)(2,1)}) custom-call(bf16[8,512,512]{2,1,0:T(8,128)(2,1)} %bitcast.189, bf16[8,32,512]{2,1,0:T(8,128)(2,1)} %pad.4.state_ref, bf16[512,1664]{1,0:T(8,128)(2,1)} %bitcast.179), custom_call_target="tpu_custom_call" | custom-call | tf_op jit(solution)/shard_map/attend/pallas_call | solution.py:152
  112.7 90.3 %feed.1 = (bf16[8,544,512]{2,1,0:T(8,128)(2,1)}, f32[8,544,512]{2,1,0:T(8,128)}, bf16[8,544,512]{2,1,0:T(8,128)(2,1)}, bf16[512,4736]{1,0:T(8,128)(2,1)}) custom-call(bf16[8,512,512]{2,1,0:T(8,128)(2,1)} %bitcast.190, bf16[8,32,512]{2,1,0:T(8,128)(2,1)} %pad.4.state_ref, bf16[512,128]{1,0:T(8,128)(2,1)} %copy-done.10, f32[1,2048]{1,0:T(1,128)} %reshape.326.upb_ref, ...), custom_call_target="tpu_custom_call" | custom-call | tf_op jit(solution)/shard_map/feed/pallas_call | solution.py:366
  203.0 4.4 %broadcast_select_fusion = (bf16[16,1,16,4736]{3,2,0,1:T(8,128)(2,1)}, bf16[16,16,4736]{2,1,0:T(8,128)(2,1)S(1)}) fusion(pred[]{:T(512)S(6)} %ne.12, bf16[16,2,16,4736]{3,2,1,0:T(8,128)(2,1)} %bitcast.198), kind=kLoop, calls=%fused_computation.9 | loop fusion | flops 2424832 | bytes 9699329 | tf_op jit(solution)/shard_map/jit(_where)/select_n | solution.py:744
  207.6 10.6 %go_back.5.refs_0_.dj_ref = bf16[1,544,1536]{2,1,0:T(8,128)(2,1)S(1)} custom-call(bf16[8,544,1536]{2,1,0:T(8,128)(2,1)} %get-tuple-element.111.qkv_ref, bf16[8,8,768,256]{3,2,1,0:T(8,128)(2,1)} %get-tuple-element.96.pt_ref, bf16[8,256,512]{2,1,0:T(8,128)(2,1)S(1)} %copy-done.3, bf16[8,544,256]{2,1,0:T(8,128)(2,1)S(1)} %copy-done.2, ...), custom_call_target="tpu_custom_call" | custom-call | flops 10000000000 | bytes 10000000 | tf_op jit(solution)/shard_map/go_back/pallas_call | solution.py:502
  218.2 2.9 convert_add_fusion
  221.3 0.5 collective-permute-start.6
  221.8 28.1 %go_back.6.refs_1_.dj_ref = bf16[3,544,1536]{2,1,0:T(8,128)(2,1)} custom-call(bf16[8,544,1536]{2,1,0:T(8,128)(2,1)} %get-tuple-element.111.qkv_ref, bf16[8,8,768,256]{3,2,1,0:T(8,128)(2,1)} %get-tuple-element.96.pt_ref, bf16[8,256,512]{2,1,0:T(8,128)(2,1)S(1)} %copy-done.3, bf16[8,544,256]{2,1,0:T(8,128)(2,1)S(1)} %copy-done.2, ...), custom_call_target="tpu_custom_call" | custom-call | flops 30000001024 | bytes 30000000 | tf_op jit(solution)/shard_map/go_back/pallas_call | solution.py:502
  250.7 0.7 collective-permute-start.7
  251.4 19.9 %go_back.7.refs_2_.dj_ref = bf16[2,544,1536]{2,1,0:T(8,128)(2,1)} custom-call(bf16[8,544,1536]{2,1,0:T(8,128)(2,1)} %get-tuple-element.111.qkv_ref, bf16[8,8,768,256]{3,2,1,0:T(8,128)(2,1)} %get-tuple-element.96.pt_ref, bf16[8,256,512]{2,1,0:T(8,128)(2,1)S(1)} %copy-done.3, bf16[8,544,256]{2,1,0:T(8,128)(2,1)S(1)} %copy-done.2, ...), custom_call_target="tpu_custom_call" | custom-call | flops 20000000000 | bytes 20000000 | tf_op jit(solution)/shard_map/go_back/pallas_call | solution.py:502
  271.6 1.5 collective-permute-start.8
  273.2 10.8 %go_back.8.refs_3_.dj_ref = bf16[1,544,1536]{2,1,0:T(8,128)(2,1)S(1)} custom-call(bf16[8,544,1536]{2,1,0:T(8,128)(2,1)} %get-tuple-element.111.qkv_ref, bf16[8,8,768,256]{3,2,1,0:T(8,128)(2,1)} %get-tuple-element.96.pt_ref, bf16[8,256,512]{2,1,0:T(8,128)(2,1)S(1)} %copy-done.3, bf16[8,544,256]{2,1,0:T(8,128)(2,1)S(1)} %copy-done.2, ...), custom_call_target="tpu_custom_call" | custom-call | flops 10000000000 | bytes 10000000 | tf_op jit(solution)/shard_map/go_back/pallas_call | solution.py:502
  284.0 1.2 copy-done.4
  285.3 3.0 collective-permute-start.9
  288.3 10.6 %go_back.9.refs_4_.dj_ref = bf16[1,544,1536]{2,1,0:T(8,128)(2,1)S(1)} custom-call(bf16[8,544,1536]{2,1,0:T(8,128)(2,1)} %get-tuple-element.111.qkv_ref, bf16[8,8,768,256]{3,2,1,0:T(8,128)(2,1)} %get-tuple-element.96.pt_ref, bf16[8,256,512]{2,1,0:T(8,128)(2,1)S(1)} %copy-done.3, bf16[8,544,256]{2,1,0:T(8,128)(2,1)S(1)} %copy-done.2, ...), custom_call_target="tpu_custom_call" | custom-call | flops 10000000000 | bytes 10000000 | tf_op jit(solution)/shard_map/go_back/pallas_call | solution.py:502
  299.0 1.6 copy-done.5
  300.6 15.4 %weigh.1 = bf16[512,1664]{1,0:T(8,128)(2,1)} custom-call(bf16[8,512,512]{2,1,0:T(8,128)(2,1)} %bitcast.191, bf16[8,32,512]{2,1,0:T(8,128)(2,1)S(1)} %copy-done.9, f32[8,544,512]{2,1,0:T(8,128)} %get-tuple-element.92.one_ref, bf16[512,1664]{1,0:T(8,128)(2,1)} %bitcast.180, bf16[1,544,1536]{2,1,0:T(8,128)(2,1)S(1)} %go_back.5.refs_0_.dj_ref, ...), custom_call_target="tpu_custom_call" | custom-call | flops 8000000000 | bytes 24000000 | tf_op jit(solution)/shard_map/weigh/pallas_call | solution.py:586
  316.0 1.2 copy-done.6
  317.1 1.7 broadcast_select_fusion.1
  319.1 2.0 descend.5.rest_0_
  321.1 4.3 %descend.6.rest_0_ = f32[8,512,512]{2,1,0:T(8,128)} custom-call(f32[8,544,512]{2,1,0:T(8,128)S(1)} %bitcast.177, bf16[3,544,1536]{2,1,0:T(8,128)(2,1)S(1)} %bitcast.187, bf16[512,1664]{1,0:T(8,128)(2,1)S(1)} %bitcast.182, f32[8,512,512]{2,1,0:T(8,128)} %descend.5.rest_0_), custom_call_target="tpu_custom_call", output_to_operand_aliasing={{}: (3, {})} | custom-call | flops 3000000000 | bytes 12000000 | tf_op jit(solution)/shard_map/descend/pallas_call | solution.py:627
  325.7 1.2 collective-permute-start.11
  326.9 0.4 copy-done.8
  327.3 3.0 descend.7.rest_0_
  330.3 2.0 descend.8.rest_0_
  332.3 2.0 descend.9
  334.4 3.4 collective-permute-done.11
  337.9 0.7 fusion.6
  338.6 0.8 slice_select_fusion.3
  339.7 1.0 collective-permute-start.12
  340.7 1.1 pad_maximum_fusion
  341.8 5.4 %copy.102 = bf16[4,2,532,512]{3,1,2,0:T(2,128)(2,1)} copy(bf16[4,2,532,512]{3,2,1,0:T(8,128)(2,1)S(1)} %bitcast.192) | data formatting | bytes 8716288 | tf_op jit(solution)/shard_map/reshape | solution.py:864
  347.3 1.2 copy_add_fusion.1
  348.9 4.3 %collective-permute-done.13 = bf16[2,16,1664]{2,1,0:T(8,128)(2,1)S(1)} collective-permute-done((bf16[2,16,1664]{2,1,0:T(8,128)(2,1)S(1)}, bf16[2,16,1664]{2,1,0:T(8,128)(2,1)S(1)}, u32[]{:S(2)}, u32[]{:S(2)}) %collective-permute-start.13) | collective-permute-done | bytes 106528 | tf_op jit(solution)/shard_map/ppermute | solution.py:716
  353.6 1.7 fusion.5.far_ref
  355.3 3.5 collective-permute-done.14
  358.8 0.7 fusion.10.near_ref
  359.4 1.8 squares.1
  361.2 1.4 collective-permute-done.15
  362.6 0.7 add.69
  363.3 1.4 collective-permute-start.16
  364.7 2.2 collective-permute-done.16
  366.9 0.8 collective-permute-start.17
  367.7 2.8 collective-permute-done.17
  370.5 3.6 collective-permute-done.18
  374.1 4.5 %collective-permute-done.19 = f32[8,128]{1,0:T(8,128)S(1)} collective-permute-done((f32[8,128]{1,0:T(8,128)S(1)}, f32[8,128]{1,0:T(8,128)S(1)}, u32[]{:S(2)}, u32[]{:S(2)}) %collective-permute-start.19) | collective-permute-done | bytes 4128 | tf_op jit(solution)/shard_map/ppermute | solution.py:716
  378.6 0.6 add.73.total_ref
  379.2 2.6 adam.1
  381.9 1.2 slice.127
  (97 shorter events, 5.0 us)
Async XLA Ops:
  7.2 105.5 %all-gather.2.cloned.1.call-start = ((), (), s32[]{:S(2)}) async-start(), calls=%async_computation | async-start | bytes 4866048 | tf_op jit(solution)/shard_map/all_gather | solution.py:818
  9.0 7.0 %collective-permute-start = (bf16[1,16,1664]{2,1,0:T(8,128)(2,1)}, bf16[1,16,1664]{2,1,0:T(8,128)(2,1)S(1)}, u32[]{:S(2)}, u32[]{:S(2)}) collective-permute-start(bf16[1,16,1664]{2,1,0:T(8,128)(2,1)} %bitcast.220), channel_id=1, source_target_pairs={{0,16},{1,17},{2,18},{3,19},{4,20},{5,21},{6,22},{7,23},{8,24},{9,... | collective-permute-start | bytes 159752 | tf_op jit(solution)/shard_map/ppermute | solution.py:716
  16.9 4.8 %collective-permute-start.1 = (bf16[2,16,1664]{2,1,0:T(8,128)(2,1)S(1)}, bf16[2,16,1664]{2,1,0:T(8,128)(2,1)S(1)}, u32[]{:S(2)}, u32[]{:S(2)}) collective-permute-start(bf16[2,16,1664]{2,1,0:T(8,128)(2,1)S(1)} %maximum_bitcast_fusion), channel_id=1, source_target_pairs={{0,8},{1,9},{2,10},{3,11},{4,12},{5,13},{6,14},{7,15},{8,0},{9,1},... | collective-permute-start | bytes 319496 | tf_op jit(solution)/shard_map/ppermute | solution.py:716
  21.8 6.9 %collective-permute-start.2 = (bf16[4,16,1664]{2,1,0:T(8,128)(2,1)S(1)}, bf16[4,16,1664]{2,1,0:T(8,128)(2,1)S(1)}, u32[]{:S(2)}, u32[]{:S(2)}) collective-permute-start(bf16[4,16,1664]{2,1,0:T(8,128)(2,1)S(1)} %bitcast.208), channel_id=1, source_target_pairs={{0,4},{1,5},{2,6},{3,7},{4,0},{5,1},{6,2},{7,3},{8,12},{9,13},{10,... | collective-permute-start | bytes 638984 | tf_op jit(solution)/shard_map/ppermute | solution.py:716
  28.9 9.9 %collective-permute-start.3 = (bf16[8,16,1664]{2,1,0:T(8,128)(2,1)S(1)}, bf16[8,16,1664]{2,1,0:T(8,128)(2,1)S(1)}, u32[]{:S(2)}, u32[]{:S(2)}) collective-permute-start(bf16[8,16,1664]{2,1,0:T(8,128)(2,1)S(1)} %bitcast.205), channel_id=1, source_target_pairs={{0,2},{1,3},{2,0},{3,1},{4,6},{5,7},{6,4},{7,5},{8,10},{9,11},{10,... | collective-permute-start | bytes 1277960 | tf_op jit(solution)/shard_map/ppermute | solution.py:716
  38.7 0.9 copy-start.11
  39.0 2.4 collective-permute-start.4
  42.0 1.2 copy-start
  42.0 70.6 %copy-start.10 = (bf16[512,128]{1,0:T(8,128)(2,1)}, bf16[512,128]{1,0:T(8,128)(2,1)S(1)}, u32[]{:S(2)}) copy-start(bf16[512,128]{1,0:T(8,128)(2,1)S(1)} %slice.130.small_ref) | copy-start | bytes 393220
  203.0 4.6 %copy-start.2 = (bf16[8,544,256]{2,1,0:T(8,128)(2,1)S(1)}, bf16[8,544,256]{2,1,0:T(8,128)(2,1)}, u32[]{:S(2)}) copy-start(bf16[8,544,256]{2,1,0:T(8,128)(2,1)} %get-tuple-element.98.ptq_ref) | copy-start | bytes 6684676
  203.0 4.6 %copy-start.3 = (bf16[8,256,512]{2,1,0:T(8,128)(2,1)S(1)}, bf16[8,256,512]{2,1,0:T(8,128)(2,1)}, u32[]{:S(2)}) copy-start(bf16[8,256,512]{2,1,0:T(8,128)(2,1)} %get-tuple-element.97.ptk_ref) | copy-start | bytes 6291460
  207.4 10.7 %collective-permute-start.5 = (bf16[16,16,4736]{2,1,0:T(8,128)(2,1)S(1)}, bf16[16,16,4736]{2,1,0:T(8,128)(2,1)}, u32[]{:S(2)}, u32[]{:S(2)}) collective-permute-start(bf16[16,16,4736]{2,1,0:T(8,128)(2,1)S(1)} %get-tuple-element.149), channel_id=1, source_target_pairs={{0,1},{1,0},{2,3},{3,2},{4,5},{5,4},{6,7},{7,6},{8,9},{9,8},{10,11... | collective-permute-start | bytes 7274504 | tf_op jit(solution)/shard_map/ppermute | solution.py:716
  221.3 29.0 %collective-permute-start.6 = (bf16[8,16,4736]{2,1,0:T(8,128)(2,1)S(1)}, bf16[8,16,4736]{2,1,0:T(8,128)(2,1)S(1)}, u32[]{:S(2)}, u32[]{:S(2)}) collective-permute-start(bf16[8,16,4736]{2,1,0:T(8,128)(2,1)S(1)} %fusion), channel_id=1, source_target_pairs={{0,2},{1,3},{2,0},{3,1},{4,6},{5,7},{6,4},{7,5},{8,10},{9,11},{10,... | collective-permute-start | bytes 3637256 | tf_op jit(solution)/shard_map/ppermute | solution.py:716
  250.7 20.7 %collective-permute-start.7 = (bf16[4,16,4736]{2,1,0:T(8,128)(2,1)S(1)}, bf16[4,16,4736]{2,1,0:T(8,128)(2,1)S(1)}, u32[]{:S(2)}, u32[]{:S(2)}) collective-permute-start(bf16[4,16,4736]{2,1,0:T(8,128)(2,1)S(1)} %fusion.1), channel_id=1, source_target_pairs={{0,4},{1,5},{2,6},{3,7},{4,0},{5,1},{6,2},{7,3},{8,12},{9,13},{10,... | collective-permute-start | bytes 1818632 | tf_op jit(solution)/shard_map/ppermute | solution.py:716
  271.6 13.5 %collective-permute-start.8 = (bf16[2,16,4736]{2,1,0:T(8,128)(2,1)S(1)}, bf16[2,16,4736]{2,1,0:T(8,128)(2,1)S(1)}, u32[]{:S(2)}, u32[]{:S(2)}) collective-permute-start(bf16[2,16,4736]{2,1,0:T(8,128)(2,1)S(1)} %fusion.4), channel_id=1, source_target_pairs={{0,8},{1,9},{2,10},{3,11},{4,12},{5,13},{6,14},{7,15},{8,0},{9,1},... | collective-permute-start | bytes 909320 | tf_op jit(solution)/shard_map/ppermute | solution.py:716
  284.0 1.2 copy-start.4
  285.3 13.7 %copy-start.9 = (bf16[8,32,512]{2,1,0:T(8,128)(2,1)S(1)}, bf16[8,32,512]{2,1,0:T(8,128)(2,1)}, u32[]{:S(2)}) copy-start(bf16[8,32,512]{2,1,0:T(8,128)(2,1)} %pad.4.state_ref) | copy-start | bytes 786436
  285.3 13.6 %collective-permute-start.9 = (bf16[1,16,4736]{2,1,0:T(8,128)(2,1)S(1)}, bf16[1,16,4736]{2,1,0:T(8,128)(2,1)S(1)}, u32[]{:S(2)}, u32[]{:S(2)}) collective-permute-start(bf16[1,16,4736]{2,1,0:T(8,128)(2,1)S(1)} %fusion.8), channel_id=1, source_target_pairs={{0,16},{1,17},{2,18},{3,19},{4,20},{5,21},{6,22},{7,23},{8,24},{9,... | collective-permute-start | bytes 454664 | tf_op jit(solution)/shard_map/ppermute | solution.py:716
  298.9 17.0 %copy-start.12 = (bf16[1,16,4736]{2,1,0:T(8,128)(2,1)}, bf16[1,16,4736]{2,1,0:T(8,128)(2,1)S(1)}, u32[]{:S(2)}) copy-start(bf16[1,16,4736]{2,1,0:T(8,128)(2,1)S(1)} %collective-permute-done.9) | copy-start | bytes 454660
  298.9 20.0 %slice-start = ((s8[8912896]{0:T(1024)(128)(4,1)}), s8[4194304]{0:T(1024)(128)(4,1)S(1)}, s32[]{:S(2)}) async-start(s8[8912896]{0:T(1024)(128)(4,1)} %bitcast.176), calls=%async_computation.1 | async-start | bytes 8388608
  299.0 1.6 copy-start.5
  300.6 18.4 %slice-start.1 = ((s8[8912896]{0:T(1024)(128)(4,1)}), s8[4194304]{0:T(1024)(128)(4,1)S(1)}, s32[]{:S(2)}) async-start(s8[8912896]{0:T(1024)(128)(4,1)} %bitcast.176), calls=%async_computation.2 | async-start | bytes 8388608
  300.6 18.4 %slice-start.2 = ((s8[8912896]{0:T(1024)(128)(4,1)}), s8[524288]{0:T(1024)(128)(4,1)S(1)}, s32[]{:S(2)}) async-start(s8[8912896]{0:T(1024)(128)(4,1)} %bitcast.176), calls=%async_computation.3 | async-start | bytes 1048576
  316.0 1.2 copy-start.6
  317.1 2.0 copy-start.1
  317.1 3.9 %slice-start.3 = ((s8[5013504]{0:T(1024)(128)(4,1)}), s8[4194304]{0:T(1024)(128)(4,1)S(1)}, s32[]{:S(2)}) async-start(s8[5013504]{0:T(1024)(128)(4,1)} %bitcast.186), calls=%async_computation.4 | async-start | bytes 8388608
  318.9 2.2 slice-start.4
  318.9 6.5 %collective-permute-start.10 = (bf16[16,16,1664]{2,1,0:T(8,128)(2,1)S(1)}, bf16[16,16,1664]{2,1,0:T(8,128)(2,1)S(1)}, u32[]{:S(2)}, u32[]{:S(2)}) collective-permute-start(bf16[16,16,1664]{2,1,0:T(8,128)(2,1)S(1)} %get-tuple-element.151), channel_id=1, source_target_pairs={{0,1},{1,0},{2,3},{3,2},{4,5},{5,4},{6,7},{7,6},{8,9},{9,8},{10,11... | collective-permute-start | bytes 2555912 | tf_op jit(solution)/shard_map/ppermute | solution.py:716
  325.4 1.9 copy-start.8
  325.7 12.2 %collective-permute-start.11 = (bf16[8,16,1664]{2,1,0:T(8,128)(2,1)S(1)}, bf16[8,16,1664]{2,1,0:T(8,128)(2,1)S(1)}, u32[]{:S(2)}, u32[]{:S(2)}) collective-permute-start(bf16[8,16,1664]{2,1,0:T(8,128)(2,1)S(1)} %fusion.3), channel_id=1, source_target_pairs={{0,2},{1,3},{2,0},{3,1},{4,6},{5,7},{6,4},{7,5},{8,10},{9,11},{10,... | collective-permute-start | bytes 1277960 | tf_op jit(solution)/shard_map/ppermute | solution.py:716
  330.3 2.0 copy-start.7
  330.3 9.1 %slice-start.5 = ((s8[4456448]{0:T(1024)(128)(4,1)}), s8[4194304]{0:T(1024)(128)(4,1)S(1)}, s32[]{:S(2)}) async-start(s8[4456448]{0:T(1024)(128)(4,1)} %bitcast.200), calls=%async_computation.6 | async-start | bytes 8388608
  332.3 7.1 %slice-start.6 = ((s8[4456448]{0:T(1024)(128)(4,1)}), s8[262144]{0:T(1024)(128)(4,1)S(1)}, s32[]{:S(2)}) async-start(s8[4456448]{0:T(1024)(128)(4,1)} %bitcast.200), calls=%async_computation.7 | async-start | bytes 524288
  339.7 7.5 %collective-permute-start.12 = (bf16[4,16,1664]{2,1,0:T(8,128)(2,1)}, bf16[4,16,1664]{2,1,0:T(8,128)(2,1)}, u32[]{:S(2)}, u32[]{:S(2)}) collective-permute-start(bf16[4,16,1664]{2,1,0:T(8,128)(2,1)} %fusion.6), channel_id=1, source_target_pairs={{0,4},{1,5},{2,6},{3,7},{4,0},{5,1},{6,2},{7,3},{8,12},{9,13},{10,... | collective-permute-start | bytes 638984 | tf_op jit(solution)/shard_map/ppermute | solution.py:716
  348.5 4.8 %collective-permute-start.13 = (bf16[2,16,1664]{2,1,0:T(8,128)(2,1)S(1)}, bf16[2,16,1664]{2,1,0:T(8,128)(2,1)S(1)}, u32[]{:S(2)}, u32[]{:S(2)}) collective-permute-start(bf16[2,16,1664]{2,1,0:T(8,128)(2,1)S(1)} %fusion.9), channel_id=1, source_target_pairs={{0,8},{1,9},{2,10},{3,11},{4,12},{5,13},{6,14},{7,15},{8,0},{9,1},... | collective-permute-start | bytes 319496 | tf_op jit(solution)/shard_map/ppermute | solution.py:716
  353.3 5.5 %collective-permute-start.14 = (bf16[1,16,1664]{2,1,0:T(8,128)(2,1)S(1)}, bf16[1,16,1664]{2,1,0:T(8,128)(2,1)S(1)}, u32[]{:S(2)}, u32[]{:S(2)}) collective-permute-start(bf16[1,16,1664]{2,1,0:T(8,128)(2,1)S(1)} %fusion.11), channel_id=1, source_target_pairs={{0,16},{1,17},{2,18},{3,19},{4,20},{5,21},{6,22},{7,23},{8,24},{9,... | collective-permute-start | bytes 159752 | tf_op jit(solution)/shard_map/ppermute | solution.py:716
  361.2 1.4 collective-permute-start.15
  363.3 3.6 collective-permute-start.16
  366.9 3.6 collective-permute-start.17
  370.5 3.6 collective-permute-start.18
  374.1 4.5 %collective-permute-start.19 = (f32[8,128]{1,0:T(8,128)S(1)}, f32[8,128]{1,0:T(8,128)S(1)}, u32[]{:S(2)}, u32[]{:S(2)}) collective-permute-start(f32[8,128]{1,0:T(8,128)S(1)} %add.72), channel_id=1, source_target_pairs={{0,16},{1,17},{2,18},{3,19},{4,20},{5,21},{6,22},{7,23},{8,24},{9,... | collective-permute-start | bytes 12296 | tf_op jit(solution)/shard_map/ppermute | solution.py:716
Sparse Core Ops, SparseCore 0:
  11.5 66.3 all-gather.1
